TPU v7x, 128 devices: a whole 4x4x4 slice. The times are simulated.
128 devices in a mesh: seq: 128 (over z, x, y, core).
Axes of the slice: x: 4, y: 4, z: 4, core: 2. Of those that a mesh axis runs over, the one named last changes fastest.
Arguments:
- queries: bfloat16 [49152, 768], P('seq'), may hold values from -6 to 6
- keys: bfloat16 [49152, 768], P('seq'), may hold values from -6 to 6
- values: bfloat16 [49152, 768], P('seq'), may hold values from -6 to 6
- grad_out: bfloat16 [49152, 768], P('seq'), may hold values from -18 to 18
- offsets: int32 [3, 12], replicated, may hold values from 0 to 127, as said below
Outputs:
- attended: bfloat16 [49152, 768], P('seq')
- grad_queries: bfloat16 [49152, 768], P('seq')
- grad_keys: bfloat16 [49152, 768], P('seq')
- grad_values: bfloat16 [49152, 768], P('seq')
Inputs may be any that keep to these rules, and one draw needn't show every extreme that they name: Row b of offsets holds the offsets of dilated branch b + 1; each entry is below that branch's dilation, and every row holds 0 and its dilation minus one.
All inputs are finite; a program needn't handle non-finite values.
Results may differ from a plain program's by a relative error of at most 0.0051.
Values may be sent and summed in bfloat16 or wider, within the bound.
No kernel may reach another device: no remote copies, remote signals or barrier semaphores. Data moves between devices by JAX's collectives and lax.ppermute only.
A program may use at most 128 MiB of HBM per device.

v0:
```python
import jax
import jax.numpy as jnp
from jax import lax
from jax.experimental import pallas as pl
from jax.experimental.pallas import tpu as pltpu
from jax.sharding import PartitionSpec as P

HEADS = 12
HEAD_DIM = 64
PAIRS = 6
LANES = 128
WIDTH = 768
TOK = 384
SPAN_NEAR = 4
SPAN_MID = 32
SPAN_ALL = 128
SPANS = (SPAN_NEAR, SPAN_MID, SPAN_ALL)
NEAR = TOK // SPAN_NEAR
MID = TOK // SPAN_MID
FAR = TOK // SPAN_ALL
MID_SLOT = 2 * MID
FAR_SLOT = 8
SHIFTS = (2, 5, 7)
CHUNKS = 2
CHIPS = 64
PLANE = 16
SCALE = 0.125
NEGATIVE = -1e30
F32 = jnp.float32
BF16 = jnp.bfloat16


def iota(shape, axis):
    return lax.broadcasted_iota(jnp.int32, shape, axis)


def nt(a, b):
    return lax.dot_general(a, b, (((1,), (1,)), ((), ())), preferred_element_type=F32)


def nn(a, b):
    return lax.dot_general(a, b, (((1,), (0,)), ((), ())), preferred_element_type=F32)


def tn(a, b):
    return lax.dot_general(a, b, (((0,), (0,)), ((), ())), preferred_element_type=F32)


def one_hot(test):
    return jnp.where(test, 1.0, 0.0).astype(BF16)


def thirds(x):
    first = x.astype(BF16)
    rest = x - first.astype(F32)
    second = rest.astype(BF16)
    return first, second, (rest - second.astype(F32)).astype(BF16)


def exact_nn(x, pick):
    rows = x.shape[0]
    y = nn(jnp.concatenate(thirds(x), axis=0), pick)
    return y[0:rows] + y[rows : 2 * rows] + y[2 * rows :]


def halves(x):
    hi = x.astype(BF16)
    return hi, (x - hi.astype(F32)).astype(BF16)


def offset_row(offsets_ref, branch):
    head = iota((1, WIDTH), 1) >> 6
    row = jnp.zeros((1, WIDTH), jnp.int32)
    for h in range(HEADS):
        row = jnp.where(head == h, offsets_ref[branch, h], row)
    return row


def offset_column(offsets_ref, branch):
    head = iota((16, 1), 0)
    column = jnp.zeros((16, 1), jnp.int32)
    for h in range(HEADS):
        column = jnp.where(head == h, offsets_ref[branch, h], column)
    return column


def head_taken(offsets_ref):
    token = iota((16, TOK), 1)
    return [(token & (SPANS[b] - 1)) == offset_column(offsets_ref, b) for b in range(3)]


def pair_block(x):
    lane = iota(x.shape, 1)
    zero = jnp.zeros((), x.dtype)
    return jnp.concatenate(
        [jnp.where(lane < HEAD_DIM, x, zero), jnp.where(lane >= HEAD_DIM, x, zero)], axis=0
    )


def head_lanes():
    return iota((HEADS, 1, WIDTH), 2) >> 6 == iota((HEADS, 1, WIDTH), 0)


def head_block(x, slots):
    return jnp.where(head_lanes(), x[None], 0.0).reshape(HEADS * slots, WIDTH).astype(BF16)


def head_sum(x, slots):
    return jnp.sum(jnp.where(head_lanes(), x.reshape(HEADS, slots, WIDTH), 0.0), axis=0)


def stat_up(rows, slots, shift):
    count = HEADS * slots
    bits = slots.bit_length() - 1
    own = iota((16, count), 1) >> bits == iota((16, count), 0)
    wide = jnp.concatenate([jnp.where(own, r, 0.0) for r in rows], axis=0)
    up = one_hot((iota((count, TOK), 0) & (slots - 1)) == iota((count, TOK), 1) >> shift)
    y = exact_nn(wide, up)
    return [y[16 * i : 16 * (i + 1)] for i in range(len(rows))]


def stat_down(xs, slots, shift):
    count = HEADS * slots
    bits = slots.bit_length() - 1
    down = one_hot(iota((TOK, count), 0) >> shift == (iota((TOK, count), 1) & (slots - 1)))
    wide = exact_nn(jnp.concatenate(xs, axis=0), down)
    keep = iota((16, count), 1) >> bits == iota((16, count), 0)
    return [
        jnp.sum(jnp.where(keep, wide[16 * i : 16 * (i + 1)], 0.0), axis=0, keepdims=True)
        for i in range(len(xs))
    ]


def spread_t(x, slots, shift):
    both = jnp.concatenate(halves(x), axis=0)
    up = one_hot(
        (iota((2 * slots, TOK), 0) & (slots - 1)) == iota((2 * slots, TOK), 1) >> shift
    )
    return tn(both, up)


def spread_tok(x, slots, shift):
    hi, lo = halves(x)
    up = one_hot(iota((TOK, slots), 1) == iota((TOK, slots), 0) >> shift)
    if slots < 64:
        return nn(jnp.concatenate([up, up], axis=1), jnp.concatenate([hi, lo], axis=0))
    return nn(up, hi) + nn(up, lo)


def spread_near_t(x):
    up = one_hot((iota((2 * LANES, TOK), 0) & (LANES - 1)) == iota((2 * LANES, TOK), 1) >> 2)
    return nn(jnp.concatenate(halves(x), axis=1), up)


def in_slots(rows, slot_rows, low, high, columns):
    slot = iota((rows // slot_rows, slot_rows, columns), 1)
    return ((slot >= low) & (slot < high)).reshape(rows, columns)


def call(
    body, out_shape, scratch=(), n_in=0, smem=(0,), cost=5, hbm=(), hbm_out=(), held=(), held_out=(),
    kept=(), kept_out=(),
):
    places = []
    for i in range(n_in):
        space = pltpu.SMEM if i in smem else pltpu.HBM if i in hbm else pltpu.VMEM
        places.append(pl.BlockSpec(memory_space=space))
    outs = [
        pl.BlockSpec(memory_space=pltpu.HBM if i in hbm_out else pltpu.VMEM)
        for i in range(len(out_shape))
    ]
    low_out = set(hbm_out) | set(held_out)
    shapes = []
    for i, x in enumerate(out_shape):
        space = pltpu.HBM if i in low_out else pltpu.VMEM if i in kept_out else None
        shapes.append(x if space is None else space(x.shape, x.dtype))
    kernel = pl.pallas_call(
        body,
        out_shape=shapes,
        in_specs=places,
        out_specs=outs,
        scratch_shapes=list(scratch),
        compiler_params=pltpu.CompilerParams(vmem_limit_bytes=16 * 1024 * 1024),
        cost_estimate=pl.CostEstimate(
            flops=cost * 1000000000, bytes_accessed=cost * 3000000, transcendentals=0
        ),
    )
    low = set(hbm) | set(held)

    def run(*operands):
        placed = []
        for i, x in enumerate(operands):
            space = pltpu.HBM if i in low else pltpu.VMEM if i in kept else None
            placed.append(x if space is None else pltpu.with_memory_space_constraint(x, space))
        return kernel(*placed)

    return run


def token_copies(sources, targets, sems):
    copies = []
    step = TOK // CHUNKS
    for a, (src, dst) in enumerate(zip(sources, targets)):
        for c in range(CHUNKS):
            rows = pl.ds(c * step, step)
            copies.append(
                pltpu.make_async_copy(src.at[rows, :], dst.at[rows, :], sems.at[a, c])
            )
            copies[-1].start()
    return copies


def wait(copies):
    for c in copies:
        c.wait()


def shape(rows, cols, dtype):
    return jax.ShapeDtypeStruct((rows, cols), dtype)


def select_body(
    off, q, k, v, g, near_kv, near_qg, mid_kvqg, far_kv, far_qg, own, vq, vk, vv,
    vg, wide, tmp, sems, near, far_tile, out_sems,
):
    staged = (vk, vv, vq, vg)
    copies = token_copies((k, v, q, g), staged, sems)
    first = iota((1, LANES), 1) < HEAD_DIM
    valid = iota((8, WIDTH), 0) < 2 * FAR
    tmp[...] = jnp.zeros((64, WIDTH), F32)
    outs = []
    for a in range(4):
        wait(copies[a * CHUNKS : (a + 1) * CHUNKS])
        for p in range(PAIRS):
            lanes = slice(p * LANES, (p + 1) * LANES)
            h = 2 * p
            base = (a * PAIRS + p) * TOK
            wide[base : base + TOK, :] = staged[a][:, lanes].astype(F32)
            a0 = wide[pl.ds(base + off[0, h], NEAR, stride=SPAN_NEAR), :]
            a1 = wide[pl.ds(base + off[0, h + 1], NEAR, stride=SPAN_NEAR), :]
            near[a * NEAR : (a + 1) * NEAR, lanes] = jnp.where(first, a0, a1).astype(BF16)
            for i in range(MID):
                b0 = wide[pl.ds(base + off[1, h] + i * SPAN_MID, 1), :]
                b1 = wide[pl.ds(base + off[1, h + 1] + i * SPAN_MID, 1), :]
                tmp[a * MID + i : a * MID + i + 1, lanes] = jnp.where(first, b0, b1)
            for i in range(FAR):
                c0 = wide[pl.ds(base + off[2, h] + i * SPAN_ALL, 1), :]
                c1 = wide[pl.ds(base + off[2, h + 1] + i * SPAN_ALL, 1), :]
                tmp[48 + a * FAR + i : 48 + a * FAR + i + 1, lanes] = jnp.where(first, c0, c1)
        if a == 1:
            kv8 = jnp.where(valid, tmp[48:56, :], 0.0)
            kv16 = jnp.concatenate([kv8, kv8], axis=0).astype(BF16)
            for d in range(CHIPS // 2):
                far_tile[d * 16 : (d + 1) * 16, :] = kv16
            outs.append(pltpu.make_async_copy(far_tile, far_kv, out_sems.at[2]))
            outs[-1].start()
        if a % 2 == 1:
            part = a // 2
            outs.append(
                pltpu.make_async_copy(
                    near.at[pl.ds(part * 2 * NEAR, 2 * NEAR), :],
                    (near_kv, near_qg)[part],
                    out_sems.at[part],
                )
            )
            outs[-1].start()
    mid_kvqg[...] = tmp[0:48, :].astype(BF16)
    far_qg[...] = jnp.concatenate([jnp.where(valid, tmp[54:62, :], 0.0)] * 2, axis=0).astype(BF16)
    row = iota((16, WIDTH), 0)
    for a in range(4):
        own[a * 16 : (a + 1) * 16, :] = jnp.where(
            row < MID, tmp[a * MID : a * MID + 16, :], 0.0
        ).astype(BF16)
        part = tmp[48 + a * FAR : 48 + a * FAR + 3, :]
        part = jnp.concatenate([part, jnp.zeros((13, WIDTH), F32)], axis=0)
        own[64 + a * 16 : 64 + (a + 1) * 16, :] = part.astype(BF16)
    wait(outs)


def local_forward_body(q, k, v, out_t, peak, total):
    peak[...] = jnp.zeros((16, TOK), F32)
    total[...] = jnp.ones((16, TOK), F32)
    for p in range(PAIRS):
        lanes = slice(p * LANES, (p + 1) * LANES)
        s = SCALE * nt(k[:, lanes], pair_block(q[:, lanes]))
        m = jnp.max(s, axis=0, keepdims=True)
        w = jnp.exp(s - m)
        t = jnp.sum(w, axis=0, keepdims=True)
        o = tn(v[:, lanes], w.astype(BF16))
        for e in range(2):
            cols = slice(e * TOK, (e + 1) * TOK)
            rows = slice(p * LANES + e * HEAD_DIM, p * LANES + (e + 1) * HEAD_DIM)
            out_t[rows, :] = o[e * HEAD_DIM : (e + 1) * HEAD_DIM, cols]
            peak[2 * p + e : 2 * p + e + 1, :] = m[:, cols]
            total[2 * p + e : 2 * p + e + 1, :] = t[:, cols]


def near_pair(refs, part, lanes):
    return jnp.concatenate([r[part * NEAR : (part + 1) * NEAR, lanes] for r in refs], axis=0)


def near_queries(ref, part, lanes):
    x = ref[part * NEAR : (part + 1) * NEAR, lanes]
    return pair_block(jnp.concatenate([x, jnp.zeros((LANES - NEAR, LANES), x.dtype)], axis=0))


def near_forward_body(qg, kv0, kv1, kv2, kv3, out_t, peak, total):
    refs = (kv0, kv1, kv2, kv3)
    peak[...] = jnp.zeros((16, LANES), F32)
    total[...] = jnp.ones((16, LANES), F32)
    for p in range(PAIRS):
        lanes = slice(p * LANES, (p + 1) * LANES)
        s = SCALE * nt(near_pair(refs, 0, lanes), near_queries(qg, 0, lanes))
        m = jnp.max(s, axis=0, keepdims=True)
        w = jnp.exp(s - m)
        t = jnp.sum(w, axis=0, keepdims=True)
        o = tn(near_pair(refs, 1, lanes), w.astype(BF16))
        for e in range(2):
            cols = slice(e * LANES, (e + 1) * LANES)
            rows = slice(p * LANES + e * HEAD_DIM, p * LANES + (e + 1) * HEAD_DIM)
            out_t[rows, :] = o[e * HEAD_DIM : (e + 1) * HEAD_DIM, cols]
            peak[2 * p + e : 2 * p + e + 1, :] = m[:, cols]
            total[2 * p + e : 2 * p + e + 1, :] = t[:, cols]


def far_forward(kv, query, slots, slot_rows, count):
    s = SCALE * nt(kv, head_block(query, slots))
    s = jnp.where(in_slots(s.shape[0], slot_rows, 0, count, s.shape[1]), s, NEGATIVE)
    m = jnp.max(s, axis=0, keepdims=True)
    w = jnp.exp(s - m)
    t = jnp.sum(w, axis=0, keepdims=True)
    o = tn(pltpu.roll(w, count, 0).astype(BF16), kv)
    return m, t, head_sum(o, slots)


def mid_forward_body(own, *rest):
    mids, (out2, peak2, total2) = rest[:8], rest[8:]
    m, t, o = far_forward(stack(mids), own[32:48, :].astype(F32), 16, MID_SLOT, MID)
    out2[...] = o
    peak2[...] = m
    total2[...] = t


def far_forward_body(far_a, far_b, own, out3, peak3, total3):
    far = jnp.concatenate([far_a[...], far_b[...]], axis=0)
    m, t, o = far_forward(far, own[96:112, :].astype(F32)[0:8], 8, FAR_SLOT, FAR)
    out3[...] = o
    peak3[...] = m
    total3[...] = t


def stack(refs):
    return jnp.concatenate([r[...] for r in refs], axis=0)


def merge_body(
    off, g, out0, peak0, total0, out1, peak1, total1, out2, peak2, total2,
    out3, peak3, total3, far_qg, attended, lse_ref, delta_ref, near_stat, far_send,
):
    taken = head_taken(off)
    up1 = one_hot(iota((LANES, TOK), 0) == iota((LANES, TOK), 1) >> 2)
    near = exact_nn(jnp.concatenate([peak1[...], total1[...]], axis=0), up1)
    mid = stat_up([peak2[...], total2[...]], 16, SHIFTS[1])
    far = stat_up([peak3[...], total3[...]], 8, SHIFTS[2])
    peaks = [near[0:16], mid[0], far[0]]
    totals = [near[16:32], mid[1], far[1]]
    peaks = [jnp.where(t, x, NEGATIVE) for t, x in zip(taken, peaks)]
    best = peak0[...]
    for x in peaks:
        best = jnp.maximum(best, x)
    den = total0[...] * jnp.exp(peak0[...] - best)
    for x, y, t in zip(peaks, totals, taken):
        den = den + jnp.where(t, y * jnp.exp(x - best), 0.0)
    lse = best + jnp.log(den)
    weight0 = jnp.exp(peak0[...] - lse)
    weights = [jnp.where(t, jnp.exp(x - lse), 0.0) for x, t in zip(peaks, taken)]
    s1 = spread_near_t(out1[...])
    s2 = spread_t(out2[...], 16, SHIFTS[1])
    s3 = spread_t(out3[...], 8, SHIFTS[2])
    parts = []
    for h in range(HEADS):
        rows = slice(h * HEAD_DIM, (h + 1) * HEAD_DIM)
        one = slice(h, h + 1)
        parts.append(
            out0[rows, :] * weight0[one]
            + s1[rows] * weights[0][one]
            + s2[rows] * weights[1][one]
            + s3[rows] * weights[2][one]
        )
    att = jnp.concatenate(parts, axis=0).T.astype(BF16)
    attended[...] = att
    hi, lo = halves(g[...].astype(F32) * att.astype(F32))
    pick = one_hot(iota((16, WIDTH), 1) >> 6 == iota((16, WIDTH), 0))
    delta = nt(pick, hi) + nt(pick, lo)
    lse_ref[...] = lse
    delta_ref[...] = delta
    down1 = one_hot(iota((TOK, LANES), 1) == iota((TOK, LANES), 0) >> 2)
    near_stat[...] = exact_nn(
        jnp.concatenate([jnp.where(taken[0], lse, 0.0), jnp.where(taken[0], delta, 0.0)], axis=0),
        down1,
    )
    column = iota((TOK, 256), 1) & 15
    row = iota((TOK, 256), 0)
    down2 = one_hot(row >> SHIFTS[1] == column)
    down3 = one_hot((row >> SHIFTS[2]) + MID == column)
    wide = exact_nn(
        jnp.concatenate([jnp.where(taken[1], lse, 0.0), jnp.where(taken[1], delta, 0.0)], axis=0),
        down2,
    ) + exact_nn(
        jnp.concatenate([jnp.where(taken[2], lse, 0.0), jnp.where(taken[2], delta, 0.0)], axis=0),
        down3,
    )
    keep = iota((16, 256), 1) >> 4 == iota((16, 256), 0)
    lines = []
    for e in range(2):
        line = jnp.sum(jnp.where(keep, wide[16 * e : 16 * e + 16], 0.0), axis=0, keepdims=True)
        lines.append(jnp.concatenate([x.astype(F32) for x in thirds(line)], axis=1))
    r = iota((16, WIDTH), 0) & 7
    send = jnp.where(r == 6, lines[0], jnp.where(r == 7, lines[1], far_qg[...].astype(F32)))
    send = send.astype(BF16)
    for d in range(CHIPS // 2):
        far_send[d * 16 : (d + 1) * 16, :] = send


def far_query_grad(kv, query, grad, lse, delta, slots, slot_rows, count):
    s = SCALE * nt(kv, head_block(query, slots))
    valid = in_slots(s.shape[0], slot_rows, 0, count, s.shape[1])
    prob = jnp.exp(jnp.where(valid, s - lse, NEGATIVE))
    dp = nt(kv, head_block(grad, slots))
    dp = pltpu.roll(dp, dp.shape[0] - count, 0)
    ds = jnp.where(valid, prob * (dp - delta), 0.0).astype(BF16)
    return SCALE * head_sum(tn(ds, kv), slots)


def local_grad_body(
    off, q_hbm, k_hbm, v_hbm, g_hbm, qg, kv0, kv1, kv2, kv3, far_a, far_b, own, lse, delta,
    near_stat, *rest
):
    mids, (grad_q, dk, dv, near_t, q, k, v, g, sems) = rest[:8], rest[8:]
    copies = token_copies((q_hbm, k_hbm, v_hbm, g_hbm), (q, k, v, g), sems)
    refs = (kv0, kv1, kv2, kv3)
    for p in range(PAIRS):
        lanes = slice(p * LANES, (p + 1) * LANES)
        h = 2 * p
        lr = jnp.concatenate([near_stat[h : h + 1, :], near_stat[h + 1 : h + 2, :]], axis=1)
        dr = jnp.concatenate([near_stat[16 + h : 17 + h, :], near_stat[17 + h : 18 + h, :]], axis=1)
        keys = near_pair(refs, 0, lanes)
        prob = jnp.exp(SCALE * nt(keys, near_queries(qg, 0, lanes)) - lr)
        dp = nt(near_pair(refs, 1, lanes), near_queries(qg, 1, lanes))
        ds = (prob * (dp - dr)).astype(BF16)
        dq = SCALE * tn(keys, ds)
        for e in range(2):
            rows = slice(p * LANES + e * HEAD_DIM, p * LANES + (e + 1) * HEAD_DIM)
            near_t[rows, :] = dq[e * HEAD_DIM : (e + 1) * HEAD_DIM, e * LANES : (e + 1) * LANES]
    taken = head_taken(off)
    far = jnp.concatenate([far_a[...], far_b[...]], axis=0)
    down = []
    for b, slots in ((1, 16), (2, 8)):
        down += stat_down([jnp.where(taken[b], x[...], 0.0) for x in (lse, delta)], slots, SHIFTS[b])
    dq2 = far_query_grad(
        stack(mids), own[32:48, :].astype(F32), own[48:64, :].astype(F32),
        down[0], down[1], 16, MID_SLOT, MID,
    )
    dq3 = far_query_grad(
        far, own[96:112, :].astype(F32)[0:8], own[112:128, :].astype(F32)[0:8],
        down[2], down[3], 8, FAR_SLOT, FAR,
    )
    s1 = spread_near_t(near_t[...])
    s2 = spread_t(dq2, 16, SHIFTS[1])
    s3 = spread_t(dq3, 8, SHIFTS[2])
    wait(copies)
    for p in range(PAIRS):
        lanes = slice(p * LANES, (p + 1) * LANES)
        qb = pair_block(q[:, lanes])
        gb = pair_block(g[:, lanes])
        lr = jnp.concatenate([lse[2 * p : 2 * p + 1, :], lse[2 * p + 1 : 2 * p + 2, :]], axis=1)
        dr = jnp.concatenate([delta[2 * p : 2 * p + 1, :], delta[2 * p + 1 : 2 * p + 2, :]], axis=1)
        prob = jnp.exp(SCALE * nt(k[:, lanes], qb) - lr)
        ds = (prob * (nt(v[:, lanes], gb) - dr)).astype(BF16)
        dv[p * TOK : (p + 1) * TOK, :] = nn(prob.astype(BF16), gb)
        dk[p * TOK : (p + 1) * TOK, :] = SCALE * nn(ds, qb)
        dq = SCALE * tn(k[:, lanes], ds)
        parts = []
        for e in range(2):
            h = 2 * p + e
            rows = slice(h * HEAD_DIM, (h + 1) * HEAD_DIM)
            total = dq[e * HEAD_DIM : (e + 1) * HEAD_DIM, e * TOK : (e + 1) * TOK]
            for t, x in zip(taken, (s1, s2, s3)):
                total = total + jnp.where(t[h : h + 1], x[rows], 0.0)
            parts.append(total)
        grad_q[:, lanes] = jnp.concatenate(parts, axis=0).T.astype(BF16)


def near_key_body(
    kv, qg0, qg1, qg2, qg3, st0, st1, st2, st3, dk_near, dv_near
):
    for p in range(PAIRS):
        lanes = slice(p * LANES, (p + 1) * LANES)
        kb = pair_block(kv[0:NEAR, lanes])
        vb = pair_block(kv[NEAR : 2 * NEAR, lanes])
        head = iota((2 * NEAR, NEAR), 0) < NEAR
        dk = jnp.zeros((2 * NEAR, LANES), F32)
        dv = jnp.zeros((2 * NEAR, LANES), F32)
        for qg, st in ((qg0, st0), (qg1, st1), (qg2, st2), (qg3, st3)):
            h = 2 * p
            queries = qg[0:NEAR, lanes]
            grads = qg[NEAR : 2 * NEAR, lanes]
            lr = jnp.where(head, st[h : h + 1, 0:NEAR], st[h + 1 : h + 2, 0:NEAR])
            dr = jnp.where(head, st[16 + h : 17 + h, 0:NEAR], st[17 + h : 18 + h, 0:NEAR])
            prob = jnp.exp(SCALE * nt(kb, queries) - lr)
            ds = (prob * (nt(vb, grads) - dr)).astype(BF16)
            dk = dk + nn(ds, queries)
            dv = dv + nn(prob.astype(BF16), grads)
        first = iota((NEAR, LANES), 1) < HEAD_DIM
        dk_near[:, lanes] = SCALE * jnp.where(first, dk[0:NEAR], dk[NEAR:])
        dv_near[:, lanes] = jnp.where(first, dv[0:NEAR], dv[NEAR:])


def stat_expand(line, slot_rows, first, low, count, slots):
    devices = line.shape[0]
    slot = iota((1, slot_rows, WIDTH), 1) - low
    mask = ((iota((1, slot_rows, WIDTH), 2) & 15) == slot + first) & (slot >= 0) & (slot < count)
    x = jnp.where(mask, line[:, None, :], 0.0).reshape(devices * slot_rows, WIDTH).astype(BF16)
    columns = HEADS * slots
    bits = slots.bit_length() - 1
    pick = one_hot(
        (iota((WIDTH, columns), 0) & 255) >> 4 == iota((WIDTH, columns), 1) >> bits
    )
    return nn(x, pick)


def far_key_grad(qg, key, value, lse, delta, slots, slot_rows, count):
    rows = qg.shape[0]
    s = SCALE * nt(qg, head_block(key, slots))
    valid = in_slots(rows, slot_rows, 0, count, s.shape[1])
    prob = jnp.exp(jnp.where(valid, s - lse, NEGATIVE))
    dp = nt(qg, head_block(value, slots))
    dp = pltpu.roll(dp, rows - count, 0)
    ds = jnp.where(valid, prob * (dp - delta), 0.0).astype(BF16)
    dk = SCALE * head_sum(tn(ds, qg), slots)
    dv = head_sum(tn(pltpu.roll(prob, count, 0).astype(BF16), qg), slots)
    return dk, dv


def key_grad_body(off, place, dk0, dv0, dk1, dv1, far_a, far_b, own, *rest):
    mids, (grad_k_hbm, grad_v_hbm, grad_k, grad_v, sems) = rest[:8], rest[8:]
    far = jnp.concatenate([far_a[...], far_b[...]], axis=0)
    own32 = own[...].astype(F32)
    line = iota((64, 2 * CHIPS * FAR_SLOT), 0)
    chip = (line & 15) ^ place[0]
    source = ((line >> 4) & 1) * (CHIPS * FAR_SLOT) + chip * FAR_SLOT + 6 + (line >> 5)
    lines2 = nn(one_hot(iota(line.shape, 1) == source), far)
    lines3 = far.astype(F32).reshape(2 * CHIPS, FAR_SLOT, WIDTH)
    lse2 = stat_expand(lines2[0:32], MID_SLOT, 0, 0, MID, 16)
    delta2 = stat_expand(lines2[32:64], MID_SLOT, 0, 0, MID, 16)
    dk2, dv2 = far_key_grad(stack(mids), own32[0:16], own32[16:32], lse2, delta2, 16, MID_SLOT, MID)
    lse3 = stat_expand(lines3[:, 6, :], FAR_SLOT, MID, 0, FAR, 8)
    delta3 = stat_expand(lines3[:, 7, :], FAR_SLOT, MID, 0, FAR, 8)
    dk3, dv3 = far_key_grad(far, own32[64:72], own32[80:88], lse3, delta3, 8, FAR_SLOT, FAR)
    token = iota((TOK, WIDTH), 0)
    taken = [(token & (SPANS[b] - 1)) == offset_row(off, b) for b in range(3)]
    outs = []
    for out, hbm, base, one, two, three in (
        (grad_k, grad_k_hbm, dk0, dk1, dk2, dk3),
        (grad_v, grad_v_hbm, dv0, dv1, dv2, dv3),
    ):
        total = jnp.concatenate([base[p * TOK : (p + 1) * TOK, :] for p in range(PAIRS)], axis=1)
        total = total + jnp.where(taken[0], spread_tok(one[...], NEAR, SHIFTS[0]), 0.0)
        total = total + jnp.where(taken[1], spread_tok(two, 16, SHIFTS[1]), 0.0)
        total = total + jnp.where(taken[2], spread_tok(three, 8, SHIFTS[2]), 0.0)
        out[...] = total.astype(BF16)
        outs.append(pltpu.make_async_copy(out, hbm, sems.at[len(outs)]))
        outs[-1].start()
    wait(outs)


def flip(value, mask):
    pairs = [(source, source ^ mask) for source in range(lax.axis_size("seq"))]
    return lax.ppermute(value, "seq", pairs)


def exchange(value, groups):
    return lax.all_to_all(value, "seq", 0, 0, tiled=True, axis_index_groups=groups)


def near_first(value):
    return value, flip(value, 1), flip(value, 2)


def near_direct(value):
    return value, flip(value, 1), flip(value, 2), flip(value, 3)


def near_second(values):
    return tuple(values) + (flip(values[2], 1),)


def near_gather(value):
    return near_second(near_first(value))


def plane_row(block):
    return [block] + [flip(block, d) for d in (8, 16, 24)]


def after(values, *deps):
    held = lax.optimization_barrier((tuple(values), tuple(deps)))
    return held[0]


def on_device(queries, keys, values, grad_out, offsets):
    devices = lax.axis_size("seq")
    chip_groups = [list(range(c, devices, 2)) for c in range(2)]
    place = (lax.axis_index("seq") >> 1).astype(jnp.int32).reshape(1)

    near_kv, near_qg, mid_kvqg, far_rep, far_qg, own, q_in, k_in, v_in = call(
        select_body,
        [
            shape(2 * NEAR, WIDTH, BF16),
            shape(2 * NEAR, WIDTH, BF16),
            shape(2 * MID_SLOT, WIDTH, BF16),
            shape(CHIPS * FAR_SLOT, WIDTH, BF16),
            shape(16, WIDTH, BF16),
            shape(128, WIDTH, BF16),
        ]
        + [shape(TOK, WIDTH, BF16)] * 3,
        [
            pltpu.VMEM((TOK, WIDTH), BF16),
            pltpu.VMEM((4 * PAIRS * TOK + 8, LANES), F32),
            pltpu.VMEM((64, WIDTH), F32),
            pltpu.SemaphoreType.DMA((4, CHUNKS)),
            pltpu.VMEM((4 * NEAR, WIDTH), BF16),
            pltpu.VMEM((CHIPS * FAR_SLOT, WIDTH), BF16),
            pltpu.SemaphoreType.DMA((3,)),
        ],
        5,
        hbm=(1, 2, 3, 4),
        hbm_out=(0, 1, 3),
        held=(0,),
        held_out=(2, 4, 5),
        kept_out=(6, 7, 8),
    )(offsets, queries, keys, values, grad_out)

    far_a = exchange(far_rep, chip_groups)
    lines = [mid_kvqg] + [flip(mid_kvqg, d) for d in (2, 4, 6)]
    near_kvs = near_gather(near_kv)
    mid_kv = jnp.concatenate([x[:MID_SLOT] for x in lines], axis=0)
    mid_qg = jnp.concatenate([x[MID_SLOT:] for x in lines], axis=0)
    mid_kvs = plane_row(mid_kv)

    out0, peak0, total0 = call(
        local_forward_body,
        [shape(WIDTH, TOK, F32), shape(16, TOK, F32), shape(16, TOK, F32)],
        (),
        3,
        (),
        kept=(0, 1, 2),
        kept_out=(0, 1, 2),
    )(q_in, after((k_in,), mid_kv)[0], v_in)
    out1, peak1, total1 = call(
        near_forward_body,
        [shape(WIDTH, LANES, F32), shape(16, LANES, F32), shape(16, LANES, F32)],
        (),
        5,
        (),
        1,
        held=(0, 1, 2, 3, 4),
        kept_out=(0, 1, 2),
    )(after((near_qg,), peak0)[0], *near_kvs)
    near_qgs = near_first(after((near_qg,), peak0)[0])
    mid_kvs = after(mid_kvs, peak1)
    far_a = after((far_a,), *mid_kvs)[0]
    far_b = flip(far_a, 1)
    near_qgs = near_second(after(near_qgs, far_a))
    mid_qgs = plane_row(after((mid_qg,), far_a)[0])
    mid_kvs = list(mid_kvs) + [flip(x, 1) for x in mid_kvs]
    out2, peak2, total2 = call(
        mid_forward_body,
        [shape(16, WIDTH, F32), shape(1, 192, F32), shape(1, 192, F32)],
        (),
        9,
        (),
        held=tuple(range(9)),
        kept_out=(0, 1, 2),
    )(own, *mid_kvs)
    out3, peak3, total3 = call(
        far_forward_body,
        [shape(8, WIDTH, F32), shape(1, 96, F32), shape(1, 96, F32)],
        (),
        3,
        (),
        held=(0, 1, 2),
        kept_out=(0, 1, 2),
    )(far_a, far_b, after((own,), peak2)[0])
    attended, lse, delta, near_stat, far_send = call(
        merge_body,
        [
            shape(TOK, WIDTH, BF16),
            shape(16, TOK, F32),
            shape(16, TOK, F32),
            shape(32, LANES, F32),
            shape(CHIPS * FAR_SLOT, WIDTH, BF16),
        ],
        (),
        15,
        held=(0, 1, 14),
        kept=tuple(range(2, 14)),
        held_out=(0, 3, 4),
        kept_out=(1, 2),
    )(
        offsets, grad_out, out0, peak0, total0, out1, peak1, total1, out2, peak2, total2,
        out3, peak3, total3, far_qg,
    )

    back_a = exchange(far_send, chip_groups)
    near_stats = near_direct(near_stat)
    mid_qgs = after(mid_qgs, lse)
    near_qg = after((near_qg,), lse, *mid_qgs, *near_qgs)[0]
    mid_qgs = list(mid_qgs) + [flip(x, 1) for x in mid_qgs]

    grad_q, dk0, dv0 = call(
        local_grad_body,
        [
            shape(TOK, WIDTH, BF16),
            shape(PAIRS * TOK, LANES, F32),
            shape(PAIRS * TOK, LANES, F32),
        ],
        [pltpu.VMEM((WIDTH, LANES), F32)]
        + [pltpu.VMEM((TOK, WIDTH), BF16)] * 4
        + [pltpu.SemaphoreType.DMA((4, CHUNKS))],
        24,
        cost=10,
        held=(0,) + tuple(range(5, 13)) + tuple(range(15, 24)),
        hbm=(1, 2, 3, 4),
        kept=(13, 14),
        held_out=(0,),
        kept_out=(1, 2),
    )(
        offsets, queries, keys, values, grad_out, near_qg, *near_kvs, far_a, far_b, own, lse,
        delta, near_stat, *mid_kvs,
    )
    back_a = after((back_a,), grad_q, *near_stats, *mid_qgs)[0]
    back_b = flip(back_a, 1)
    dk1, dv1 = call(
        near_key_body,
        [shape(NEAR, WIDTH, F32), shape(NEAR, WIDTH, F32)],
        (),
        9,
        (),
        held=tuple(range(9)),
        kept_out=(0, 1),
    )(after((near_kv,), back_a)[0], *near_qgs, *near_stats)
    grad_k, grad_v = call(
        key_grad_body,
        [shape(TOK, WIDTH, BF16), shape(TOK, WIDTH, BF16)],
        [
            pltpu.VMEM((TOK, WIDTH), BF16),
            pltpu.VMEM((TOK, WIDTH), BF16),
            pltpu.SemaphoreType.DMA((2,)),
        ],
        17,
        (0, 1),
        hbm_out=(0, 1),
        held=tuple(range(6, 17)),
        kept=(2, 3, 4, 5),
    )(offsets, place, dk0, dv0, dk1, dv1, back_a, back_b, own, *mid_qgs)
    return attended, grad_q, grad_k, grad_v


def solution(mesh):
    placed = (P("seq", None), P("seq", None), P("seq", None), P("seq", None), P())
    return jax.shard_map(
        on_device,
        mesh=mesh,
        in_specs=placed,
        out_specs=(P("seq", None),) * 4,
        check_vma=False,
    )
```

profile of v0, /device:TPU:1, one launch (start us, length us, event | category | flops | bytes accessed | tf_op | source)
XLA Modules:
  0.0 104.0 jit_solution(6142031076025775738)
XLA Ops:
  0.6 4.4 %shard_map.84 = (bf16[192,768]{1,0:T(8,128)(2,1)}, bf16[192,768]{1,0:T(8,128)(2,1)}, bf16[48,768]{1,0:T(8,128)(2,1)}, bf16[512,768]{1,0:T(8,128)(2,1)}, bf16[16,...) custom-call(s32[3,12]{1,0:T(4,128)} %off.7, ...), custom_call_target="tpu_custom_call" | custom-call | flops 5000000000 | bytes 15000000 | tf_op jit(solution)/shard_map/pallas_call | solution.py:195
  5.0 0.0 copy-start.3
  5.0 2.2 %collective-permute-start = (bf16[48,768]{1,0:T(8,128)(2,1)}, bf16[48,768]{1,0:T(8,128)(2,1)S(1)}, u32[]{:S(2)}, u32[]{:S(2)}) collective-permute-start(bf16[48,768]{1,0:T(8,128)(2,1)} %get-tuple-element.58), channel_id=1, source_target_pairs={{0,2},{1,3},{2,0},{3,1},{4,6},{5,7},{6,4},{7,5},{8,10},{9,11},{10,... | collective-permute-start | bytes 221192 | tf_op jit(solution)/shard_map/ppermute | solution.py:579
  7.2 2.6 %collective-permute-start.1 = (bf16[48,768]{1,0:T(8,128)(2,1)}, bf16[48,768]{1,0:T(8,128)(2,1)S(1)}, u32[]{:S(2)}, u32[]{:S(2)}) collective-permute-start(bf16[48,768]{1,0:T(8,128)(2,1)} %get-tuple-element.58), channel_id=1, source_target_pairs={{0,4},{1,5},{2,6},{3,7},{4,0},{5,1},{6,2},{7,3},{8,12},{9,13},{10,... | collective-permute-start | bytes 221192 | tf_op jit(solution)/shard_map/ppermute | solution.py:579
  9.8 0.0 collective-permute-start.4
  9.9 1.8 %collective-permute-start.3 = (bf16[192,768]{1,0:T(8,128)(2,1)}, bf16[192,768]{1,0:T(8,128)(2,1)}, u32[]{:S(2)}, u32[]{:S(2)}) collective-permute-start(bf16[192,768]{1,0:T(8,128)(2,1)} %get-tuple-element.103.kv0.kv), channel_id=1, source_target_pairs={{0,1},{1,0},{2,3},{3,2},{4,5},{5,4},{6,7},{7,6},{8,9},{9,8},{10,11... | collective-permute-start | bytes 884744 | tf_op jit(solution)/shard_map/ppermute | solution.py:579
  11.7 12.3 %all-to-all-start = ((bf16[64,8,768]{2,1,0:T(8,128)(2,1)}), bf16[64,8,768]{2,1,0:T(8,128)(2,1)}, u32[]{:S(2)}, u32[]{:S(2)}) async-start(bf16[64,8,768]{2,1,0:T(8,128)(2,1)} %bitcast.5), calls=%async_computation | async-start | bytes 1572864 | tf_op jit(solution)/shard_map/all_to_all | solution.py:583
  24.1 1.0 collective-permute-start.6
  25.1 2.4 %collective-permute-start.7 = (bf16[96,768]{1,0:T(8,128)(2,1)S(1)}, bf16[96,768]{1,0:T(8,128)(2,1)}, u32[]{:S(2)}, u32[]{:S(2)}) collective-permute-start(bf16[96,768]{1,0:T(8,128)(2,1)S(1)} %pad_maximum_fusion.rest_0_), channel_id=1, source_target_pairs={{0,16},{1,17},{2,18},{3,19},{4,20},{5,21},{6,22},{7,23},{8,24},{9,... | collective-permute-start | bytes 442376 | tf_op jit(solution)/shard_map/ppermute | solution.py:579
  27.5 0.5 collective-permute-start.8
  28.0 1.1 %collective-permute-start.5 = (bf16[192,768]{1,0:T(8,128)(2,1)}, bf16[192,768]{1,0:T(8,128)(2,1)S(1)}, u32[]{:S(2)}, u32[]{:S(2)}) collective-permute-start(bf16[192,768]{1,0:T(8,128)(2,1)} %collective-permute-done.4.kv2), channel_id=1, source_target_pairs={{0,1},{1,0},{2,3},{3,2},{4,5},{5,4},{6,7},{7,6},{8,9},{9,8},{10,11... | collective-permute-start | bytes 884744 | tf_op jit(solution)/shard_map/ppermute | solution.py:579
  29.1 3.4 %shard_map.85 = (f32[768,384]{1,0:T(8,128)S(1)}, f32[16,384]{1,0:T(8,128)S(1)}, f32[16,384]{1,0:T(8,128)S(1)}) custom-call(bf16[384,768]{1,0:T(8,128)(2,1)S(1)} %get-tuple-element.56.q, bf16[384,768]{1,0:T(8,128)(2,1)S(1)} %get-tuple-element.59.k, bf16[384,768]{1,0:T(8,128)(2,1)S(1)} %get-tuple-element.60.v), custom_call_target="tpu_custom_call" | custom-call | flops 5000000000 | bytes 15000000 | tf_op jit(solution)/shard_map/pallas_call | solution.py:195
  32.6 0.0 copy-start.5
  32.6 0.7 copy-done.6
  33.3 3.3 %shard_map.86 = (f32[768,128]{1,0:T(8,128)S(1)}, f32[16,128]{1,0:T(8,128)S(1)}, f32[16,128]{1,0:T(8,128)S(1)}) custom-call(bf16[192,768]{1,0:T(8,128)(2,1)} %get-tuple-element.95.qg.qg0, bf16[192,768]{1,0:T(8,128)(2,1)} %get-tuple-element.103.kv0.kv, bf16[192,768]{1,0:T(8,128)(2,1)} %collective-permute-done.3.kv1, ...), custom_call_target="tpu_custom_call" | custom-call | flops 1000000000 | bytes 3000000 | tf_op jit(solution)/shard_map/pallas_call | solution.py:195
  36.6 0.2 collective-permute-done.6.rest_1_
  36.8 4.7 %collective-permute-done.7.rest_2_ = bf16[96,768]{1,0:T(8,128)(2,1)} collective-permute-done((bf16[96,768]{1,0:T(8,128)(2,1)S(1)}, bf16[96,768]{1,0:T(8,128)(2,1)}, u32[]{:S(2)}, u32[]{:S(2)}) %collective-permute-start.7) | collective-permute-done | bytes 147488 | tf_op jit(solution)/shard_map/ppermute | solution.py:579
  41.5 1.1 %collective-permute-start.13 = (bf16[512,768]{1,0:T(8,128)(2,1)}, bf16[512,768]{1,0:T(8,128)(2,1)S(1)}, u32[]{:S(2)}, u32[]{:S(2)}) collective-permute-start(bf16[512,768]{1,0:T(8,128)(2,1)} %bitcast.1.far_a), channel_id=1, source_target_pairs={{0,1},{1,0},{2,3},{3,2},{4,5},{5,4},{6,7},{7,6},{8,9},{9,8},{10,11... | collective-permute-start | bytes 2359304 | tf_op jit(solution)/shard_map/ppermute | solution.py:579
  42.6 0.1 collective-permute-start.10
  42.7 0.4 collective-permute-start.11
  43.1 0.1 collective-permute-start.12
  43.2 0.4 collective-permute-start.9
  43.6 1.5 %collective-permute-done.10.rest_5_ = bf16[96,768]{1,0:T(8,128)(2,1)S(1)} collective-permute-done((bf16[96,768]{1,0:T(8,128)(2,1)}, bf16[96,768]{1,0:T(8,128)(2,1)S(1)}, u32[]{:S(2)}, u32[]{:S(2)}) %collective-permute-start.10) | collective-permute-done | bytes 147488 | tf_op jit(solution)/shard_map/ppermute | solution.py:579
  45.1 0.4 collective-permute-start.17
  45.5 1.2 %collective-permute-start.18 = (bf16[192,768]{1,0:T(8,128)(2,1)S(1)}, bf16[192,768]{1,0:T(8,128)(2,1)S(1)}, u32[]{:S(2)}, u32[]{:S(2)}) collective-permute-start(bf16[192,768]{1,0:T(8,128)(2,1)S(1)} %copy-done.5), channel_id=1, source_target_pairs={{0,2},{1,3},{2,0},{3,1},{4,6},{5,7},{6,4},{7,5},{8,10},{9,11},{10,... | collective-permute-start | bytes 884744 | tf_op jit(solution)/shard_map/ppermute | solution.py:579
  46.7 0.6 copy-done.15
  47.4 0.0 copy-done.16
  47.4 2.8 %shard_map.87 = (f32[16,768]{1,0:T(8,128)S(1)}, f32[1,192]{1,0:T(1,128)S(1)}, f32[1,192]{1,0:T(1,128)S(1)}) custom-call(bf16[128,768]{1,0:T(8,128)(2,1)} %get-tuple-element.80.own, bf16[96,768]{1,0:T(8,128)(2,1)} %copy-done.1, bf16[96,768]{1,0:T(8,128)(2,1)} %collective-permute-done.6.rest_1_, bf16[96,768]{1,0:T(8,128)(2,1)} %collective-permute-done.7.rest_2_, ...), custom_call_target="tpu_custom_call" | custom-call | flops 5000000000 | bytes 15000000 | tf_op jit(solution)/shard_map/pallas_call | solution.py:195
  50.2 0.4 collective-permute-start.14
  50.6 1.8 %collective-permute-start.15 = (bf16[96,768]{1,0:T(8,128)(2,1)S(1)}, bf16[96,768]{1,0:T(8,128)(2,1)}, u32[]{:S(2)}, u32[]{:S(2)}) collective-permute-start(bf16[96,768]{1,0:T(8,128)(2,1)S(1)} %pad_maximum_fusion.1.rest_0_), channel_id=1, source_target_pairs={{0,16},{1,17},{2,18},{3,19},{4,20},{5,21},{6,22},{7,23},{8,24},{9,... | collective-permute-start | bytes 442376 | tf_op jit(solution)/shard_map/ppermute | solution.py:579
  52.4 1.8 %collective-permute-start.16 = (bf16[96,768]{1,0:T(8,128)(2,1)S(1)}, bf16[96,768]{1,0:T(8,128)(2,1)S(1)}, u32[]{:S(2)}, u32[]{:S(2)}) collective-permute-start(bf16[96,768]{1,0:T(8,128)(2,1)S(1)} %pad_maximum_fusion.1.rest_0_), channel_id=1, source_target_pairs={{0,24},{1,25},{2,26},{3,27},{4,28},{5,29},{6,30},{7,31},{8,16},{9,... | collective-permute-start | bytes 442376 | tf_op jit(solution)/shard_map/ppermute | solution.py:579
  54.2 1.4 %collective-permute-start.19 = (bf16[192,768]{1,0:T(8,128)(2,1)S(1)}, bf16[192,768]{1,0:T(8,128)(2,1)S(1)}, u32[]{:S(2)}, u32[]{:S(2)}) collective-permute-start(bf16[192,768]{1,0:T(8,128)(2,1)S(1)} %collective-permute-done.18.qg2), channel_id=1, source_target_pairs={{0,1},{1,0},{2,3},{3,2},{4,5},{5,4},{6,7},{7,6},{8,9},{9,8},{10,11... | collective-permute-start | bytes 884744 | tf_op jit(solution)/shard_map/ppermute | solution.py:579
  55.6 0.9 copy-done.4
  56.5 2.8 %shard_map.88 = (f32[8,768]{1,0:T(8,128)S(1)}, f32[1,96]{1,0:T(1,128)S(1)}, f32[1,96]{1,0:T(1,128)S(1)}) custom-call(bf16[512,768]{1,0:T(8,128)(2,1)} %bitcast.1.far_a, bf16[512,768]{1,0:T(8,128)(2,1)} %copy-done.4, bf16[128,768]{1,0:T(8,128)(2,1)} %get-tuple-element.80.own), custom_call_target="tpu_custom_call" | custom-call | flops 5000000000 | bytes 15000000 | tf_op jit(solution)/shard_map/pallas_call | solution.py:195
  59.3 3.7 %shard_map.89 = (bf16[384,768]{1,0:T(8,128)(2,1)}, f32[16,384]{1,0:T(8,128)S(1)}, f32[16,384]{1,0:T(8,128)S(1)}, f32[32,128]{1,0:T(8,128)}, bf16[512,768]{1,0:T(8,128)(2,1)}) custom-call(s32[3,12]{1,0:T(4,128)} %off.7, bf16[384,768]{1,0:T(8,128)(2,1)} %g_hbm.1, f32[768,384]{1,0:T(8,128)S(1)} %get-tuple-element.61.out0, ...), custom_call_target="tpu_custom_call" | custom-call | flops 5000000000 | bytes 15000000 | tf_op jit(solution)/shard_map/pallas_call | solution.py:195
  63.0 0.1 collective-permute-start.20
  63.1 0.6 collective-permute-start.21
  63.7 0.8 collective-permute-start.23
  64.5 0.1 collective-permute-start.24
  64.6 0.5 collective-permute-start.25
  65.1 8.2 %all-to-all-start.1 = ((bf16[64,8,768]{2,1,0:T(8,128)(2,1)}), bf16[64,8,768]{2,1,0:T(8,128)(2,1)}, u32[]{:S(2)}, u32[]{:S(2)}) async-start(bf16[64,8,768]{2,1,0:T(8,128)(2,1)} %bitcast.6), calls=%async_computation.1 | async-start | bytes 1572864 | tf_op jit(solution)/shard_map/all_to_all | solution.py:583
  73.3 0.4 collective-permute-start.26
  73.8 1.4 %collective-permute-start.22 = (f32[32,128]{1,0:T(8,128)S(1)}, f32[32,128]{1,0:T(8,128)S(1)}, u32[]{:S(2)}, u32[]{:S(2)}) collective-permute-start(f32[32,128]{1,0:T(8,128)S(1)} %copy-done.20), channel_id=1, source_target_pairs={{0,3},{1,2},{2,1},{3,0},{4,7},{5,6},{6,5},{7,4},{8,11},{9,10},{10,... | collective-permute-start | bytes 49160 | tf_op jit(solution)/shard_map/ppermute | solution.py:579
  75.2 12.6 %shard_map.90 = (bf16[384,768]{1,0:T(8,128)(2,1)}, f32[2304,128]{1,0:T(8,128)S(1)}, f32[2304,128]{1,0:T(8,128)S(1)}) custom-call(s32[3,12]{1,0:T(4,128)} %off.7, bf16[384,768]{1,0:T(8,128)(2,1)} %q_hbm.1, bf16[384,768]{1,0:T(8,128)(2,1)} %k_hbm.1, bf16[384,768]{1,0:T(8,128)(2,1)} %v_hbm.1, bf16[384,768]{1,0:T(8,128)(2,1)} %g_hbm.1, ...), custom_call_target="tpu_custom_call" | custom-call | flops 10000000000 | bytes 30000000 | tf_op jit(solution)/shard_map/pallas_call | solution.py:195
  87.9 0.6 all-to-all-done.1
  88.5 1.6 %collective-permute-start.27 = (bf16[512,768]{1,0:T(8,128)(2,1)}, bf16[512,768]{1,0:T(8,128)(2,1)}, u32[]{:S(2)}, u32[]{:S(2)}) collective-permute-start(bf16[512,768]{1,0:T(8,128)(2,1)} %bitcast.4.far_a), channel_id=1, source_target_pairs={{0,1},{1,0},{2,3},{3,2},{4,5},{5,4},{6,7},{7,6},{8,9},{9,8},{10,11... | collective-permute-start | bytes 2359304 | tf_op jit(solution)/shard_map/ppermute | solution.py:579
  90.1 4.9 %shard_map.91 = (f32[96,768]{1,0:T(8,128)S(1)}, f32[96,768]{1,0:T(8,128)S(1)}) custom-call(bf16[192,768]{1,0:T(8,128)(2,1)} %get-tuple-element.103.kv0.kv, bf16[192,768]{1,0:T(8,128)(2,1)} %get-tuple-element.95.qg.qg0, bf16[192,768]{1,0:T(8,128)(2,1)} %copy-done.7, bf16[192,768]{1,0:T(8,128)(2,1)} %copy-done.8, bf16[192,768]{1,0:T(8,128)(2,1)} %copy-done.9, ...), custom_call_target="tpu_custom_call" | custom-call | flops 5000000000 | bytes 15000000 | tf_op jit(solution)/shard_map/pallas_call | solution.py:195
  95.1 8.7 %shard_map.92 = (bf16[384,768]{1,0:T(8,128)(2,1)}, bf16[384,768]{1,0:T(8,128)(2,1)}) custom-call(s32[3,12]{1,0:T(4,128)S(1)} %copy-done, s32[1]{0:T(128)} %bitcast.2.place, f32[2304,128]{1,0:T(8,128)S(1)} %get-tuple-element.99.dk0, f32[2304,128]{1,0:T(8,128)S(1)} %get-tuple-element.100.dv0, f32[96,768]{1,0:T(8,128)S(1)} %get-tuple-element.104.dk1, ...), custom_call_target="tpu_custom_call" | custom-call | flops 5000000000 | bytes 15000000 | tf_op jit(solution)/shard_map/pallas_call | solution.py:195
  (75 shorter events, 0.2 us)
Async XLA Ops:
  5.0 19.0 %copy-start.3 = (bf16[48,768]{1,0:T(8,128)(2,1)S(1)}, bf16[48,768]{1,0:T(8,128)(2,1)}, u32[]{:S(2)}) copy-start(bf16[48,768]{1,0:T(8,128)(2,1)} %get-tuple-element.58) | copy-start | bytes 221188
  5.0 19.0 %collective-permute-start = (bf16[48,768]{1,0:T(8,128)(2,1)}, bf16[48,768]{1,0:T(8,128)(2,1)S(1)}, u32[]{:S(2)}, u32[]{:S(2)}) collective-permute-start(bf16[48,768]{1,0:T(8,128)(2,1)} %get-tuple-element.58), channel_id=1, source_target_pairs={{0,2},{1,3},{2,0},{3,1},{4,6},{5,7},{6,4},{7,5},{8,10},{9,11},{10,... | collective-permute-start | bytes 221192 | tf_op jit(solution)/shard_map/ppermute | solution.py:579
  7.2 16.8 %collective-permute-start.1 = (bf16[48,768]{1,0:T(8,128)(2,1)}, bf16[48,768]{1,0:T(8,128)(2,1)S(1)}, u32[]{:S(2)}, u32[]{:S(2)}) collective-permute-start(bf16[48,768]{1,0:T(8,128)(2,1)} %get-tuple-element.58), channel_id=1, source_target_pairs={{0,4},{1,5},{2,6},{3,7},{4,0},{5,1},{6,2},{7,3},{8,12},{9,13},{10,... | collective-permute-start | bytes 221192 | tf_op jit(solution)/shard_map/ppermute | solution.py:579
  9.8 14.2 %collective-permute-start.2 = (bf16[48,768]{1,0:T(8,128)(2,1)}, bf16[48,768]{1,0:T(8,128)(2,1)S(1)}, u32[]{:S(2)}, u32[]{:S(2)}) collective-permute-start(bf16[48,768]{1,0:T(8,128)(2,1)} %get-tuple-element.58), channel_id=1, source_target_pairs={{0,6},{1,7},{2,4},{3,5},{4,2},{5,3},{6,0},{7,1},{8,14},{9,15},{10,... | collective-permute-start | bytes 221192 | tf_op jit(solution)/shard_map/ppermute | solution.py:579
  9.8 18.2 %collective-permute-start.4 = (bf16[192,768]{1,0:T(8,128)(2,1)}, bf16[192,768]{1,0:T(8,128)(2,1)}, u32[]{:S(2)}, u32[]{:S(2)}) collective-permute-start(bf16[192,768]{1,0:T(8,128)(2,1)} %get-tuple-element.103.kv0.kv), channel_id=1, source_target_pairs={{0,2},{1,3},{2,0},{3,1},{4,6},{5,7},{6,4},{7,5},{8,10},{9,11},{10,... | collective-permute-start | bytes 884744 | tf_op jit(solution)/shard_map/ppermute | solution.py:579
  9.9 22.7 %collective-permute-start.3 = (bf16[192,768]{1,0:T(8,128)(2,1)}, bf16[192,768]{1,0:T(8,128)(2,1)}, u32[]{:S(2)}, u32[]{:S(2)}) collective-permute-start(bf16[192,768]{1,0:T(8,128)(2,1)} %get-tuple-element.103.kv0.kv), channel_id=1, source_target_pairs={{0,1},{1,0},{2,3},{3,2},{4,5},{5,4},{6,7},{7,6},{8,9},{9,8},{10,11... | collective-permute-start | bytes 884744 | tf_op jit(solution)/shard_map/ppermute | solution.py:579
  11.7 29.8 %all-to-all-start = ((bf16[64,8,768]{2,1,0:T(8,128)(2,1)}), bf16[64,8,768]{2,1,0:T(8,128)(2,1)}, u32[]{:S(2)}, u32[]{:S(2)}) async-start(bf16[64,8,768]{2,1,0:T(8,128)(2,1)} %bitcast.5), calls=%async_computation | async-start | bytes 1572864 | tf_op jit(solution)/shard_map/all_to_all | solution.py:583
  24.1 19.1 %copy-start.1 = (bf16[96,768]{1,0:T(8,128)(2,1)}, bf16[96,768]{1,0:T(8,128)(2,1)S(1)}, u32[]{:S(2)}) copy-start(bf16[96,768]{1,0:T(8,128)(2,1)S(1)} %pad_maximum_fusion.rest_0_) | copy-start | bytes 442372
  24.1 12.7 %collective-permute-start.6 = (bf16[96,768]{1,0:T(8,128)(2,1)S(1)}, bf16[96,768]{1,0:T(8,128)(2,1)}, u32[]{:S(2)}, u32[]{:S(2)}) collective-permute-start(bf16[96,768]{1,0:T(8,128)(2,1)S(1)} %pad_maximum_fusion.rest_0_), channel_id=1, source_target_pairs={{0,8},{1,9},{2,10},{3,11},{4,12},{5,13},{6,14},{7,15},{8,0},{9,1},... | collective-permute-start | bytes 442376 | tf_op jit(solution)/shard_map/ppermute | solution.py:579
  25.1 16.4 %collective-permute-start.7 = (bf16[96,768]{1,0:T(8,128)(2,1)S(1)}, bf16[96,768]{1,0:T(8,128)(2,1)}, u32[]{:S(2)}, u32[]{:S(2)}) collective-permute-start(bf16[96,768]{1,0:T(8,128)(2,1)S(1)} %pad_maximum_fusion.rest_0_), channel_id=1, source_target_pairs={{0,16},{1,17},{2,18},{3,19},{4,20},{5,21},{6,22},{7,23},{8,24},{9,... | collective-permute-start | bytes 442376 | tf_op jit(solution)/shard_map/ppermute | solution.py:579
  27.5 14.0 %collective-permute-start.8 = (bf16[96,768]{1,0:T(8,128)(2,1)S(1)}, bf16[96,768]{1,0:T(8,128)(2,1)}, u32[]{:S(2)}, u32[]{:S(2)}) collective-permute-start(bf16[96,768]{1,0:T(8,128)(2,1)S(1)} %pad_maximum_fusion.rest_0_), channel_id=1, source_target_pairs={{0,24},{1,25},{2,26},{3,27},{4,28},{5,29},{6,30},{7,31},{8,16},{9,... | collective-permute-start | bytes 442376 | tf_op jit(solution)/shard_map/ppermute | solution.py:579
  28.0 4.6 %collective-permute-start.5 = (bf16[192,768]{1,0:T(8,128)(2,1)}, bf16[192,768]{1,0:T(8,128)(2,1)S(1)}, u32[]{:S(2)}, u32[]{:S(2)}) collective-permute-start(bf16[192,768]{1,0:T(8,128)(2,1)} %collective-permute-done.4.kv2), channel_id=1, source_target_pairs={{0,1},{1,0},{2,3},{3,2},{4,5},{5,4},{6,7},{7,6},{8,9},{9,8},{10,11... | collective-permute-start | bytes 884744 | tf_op jit(solution)/shard_map/ppermute | solution.py:579
  32.6 12.6 %copy-start.5 = (bf16[192,768]{1,0:T(8,128)(2,1)S(1)}, bf16[192,768]{1,0:T(8,128)(2,1)}, u32[]{:S(2)}) copy-start(bf16[192,768]{1,0:T(8,128)(2,1)} %get-tuple-element.95.qg.qg0) | copy-start | bytes 884740
  41.5 14.1 %collective-permute-start.13 = (bf16[512,768]{1,0:T(8,128)(2,1)}, bf16[512,768]{1,0:T(8,128)(2,1)S(1)}, u32[]{:S(2)}, u32[]{:S(2)}) collective-permute-start(bf16[512,768]{1,0:T(8,128)(2,1)} %bitcast.1.far_a), channel_id=1, source_target_pairs={{0,1},{1,0},{2,3},{3,2},{4,5},{5,4},{6,7},{7,6},{8,9},{9,8},{10,11... | collective-permute-start | bytes 2359304 | tf_op jit(solution)/shard_map/ppermute | solution.py:579
  42.6 2.5 %collective-permute-start.10 = (bf16[96,768]{1,0:T(8,128)(2,1)}, bf16[96,768]{1,0:T(8,128)(2,1)S(1)}, u32[]{:S(2)}, u32[]{:S(2)}) collective-permute-start(bf16[96,768]{1,0:T(8,128)(2,1)} %collective-permute-done.6.rest_1_), channel_id=1, source_target_pairs={{0,1},{1,0},{2,3},{3,2},{4,5},{5,4},{6,7},{7,6},{8,9},{9,8},{10,11... | collective-permute-start | bytes 442376 | tf_op jit(solution)/shard_map/ppermute | solution.py:579
  42.7 2.8 %collective-permute-start.11 = (bf16[96,768]{1,0:T(8,128)(2,1)}, bf16[96,768]{1,0:T(8,128)(2,1)S(1)}, u32[]{:S(2)}, u32[]{:S(2)}) collective-permute-start(bf16[96,768]{1,0:T(8,128)(2,1)} %collective-permute-done.7.rest_2_), channel_id=1, source_target_pairs={{0,1},{1,0},{2,3},{3,2},{4,5},{5,4},{6,7},{7,6},{8,9},{9,8},{10,11... | collective-permute-start | bytes 442376 | tf_op jit(solution)/shard_map/ppermute | solution.py:579
  43.1 3.6 %collective-permute-start.12 = (bf16[96,768]{1,0:T(8,128)(2,1)}, bf16[96,768]{1,0:T(8,128)(2,1)S(1)}, u32[]{:S(2)}, u32[]{:S(2)}) collective-permute-start(bf16[96,768]{1,0:T(8,128)(2,1)} %collective-permute-done.8.rest_3_), channel_id=1, source_target_pairs={{0,1},{1,0},{2,3},{3,2},{4,5},{5,4},{6,7},{7,6},{8,9},{9,8},{10,11... | collective-permute-start | bytes 442376 | tf_op jit(solution)/shard_map/ppermute | solution.py:579
  43.2 3.5 %collective-permute-start.9 = (bf16[96,768]{1,0:T(8,128)(2,1)S(1)}, bf16[96,768]{1,0:T(8,128)(2,1)S(1)}, u32[]{:S(2)}, u32[]{:S(2)}) collective-permute-start(bf16[96,768]{1,0:T(8,128)(2,1)S(1)} %pad_maximum_fusion.rest_0_), channel_id=1, source_target_pairs={{0,1},{1,0},{2,3},{3,2},{4,5},{5,4},{6,7},{7,6},{8,9},{9,8},{10,11... | collective-permute-start | bytes 442376 | tf_op jit(solution)/shard_map/ppermute | solution.py:579
  43.6 20.1 %copy-start.2 = (bf16[96,768]{1,0:T(8,128)(2,1)}, bf16[96,768]{1,0:T(8,128)(2,1)S(1)}, u32[]{:S(2)}) copy-start(bf16[96,768]{1,0:T(8,128)(2,1)S(1)} %pad_maximum_fusion.1.rest_0_) | copy-start | bytes 442372
  45.1 1.6 %copy-start.13 = (bf16[96,768]{1,0:T(8,128)(2,1)}, bf16[96,768]{1,0:T(8,128)(2,1)S(1)}, u32[]{:S(2)}) copy-start(bf16[96,768]{1,0:T(8,128)(2,1)S(1)} %collective-permute-done.10.rest_5_) | copy-start | bytes 442372
  45.1 7.2 %collective-permute-start.17 = (bf16[192,768]{1,0:T(8,128)(2,1)S(1)}, bf16[192,768]{1,0:T(8,128)(2,1)S(1)}, u32[]{:S(2)}, u32[]{:S(2)}) collective-permute-start(bf16[192,768]{1,0:T(8,128)(2,1)S(1)} %copy-done.5), channel_id=1, source_target_pairs={{0,1},{1,0},{2,3},{3,2},{4,5},{5,4},{6,7},{7,6},{8,9},{9,8},{10,11... | collective-permute-start | bytes 884744 | tf_op jit(solution)/shard_map/ppermute | solution.py:579
  45.5 8.6 %collective-permute-start.18 = (bf16[192,768]{1,0:T(8,128)(2,1)S(1)}, bf16[192,768]{1,0:T(8,128)(2,1)S(1)}, u32[]{:S(2)}, u32[]{:S(2)}) collective-permute-start(bf16[192,768]{1,0:T(8,128)(2,1)S(1)} %copy-done.5), channel_id=1, source_target_pairs={{0,2},{1,3},{2,0},{3,1},{4,6},{5,7},{6,4},{7,5},{8,10},{9,11},{10,... | collective-permute-start | bytes 884744 | tf_op jit(solution)/shard_map/ppermute | solution.py:579
  50.2 12.9 %collective-permute-start.14 = (bf16[96,768]{1,0:T(8,128)(2,1)S(1)}, bf16[96,768]{1,0:T(8,128)(2,1)S(1)}, u32[]{:S(2)}, u32[]{:S(2)}) collective-permute-start(bf16[96,768]{1,0:T(8,128)(2,1)S(1)} %pad_maximum_fusion.1.rest_0_), channel_id=1, source_target_pairs={{0,8},{1,9},{2,10},{3,11},{4,12},{5,13},{6,14},{7,15},{8,0},{9,1},... | collective-permute-start | bytes 442376 | tf_op jit(solution)/shard_map/ppermute | solution.py:579
  50.6 13.1 %collective-permute-start.15 = (bf16[96,768]{1,0:T(8,128)(2,1)S(1)}, bf16[96,768]{1,0:T(8,128)(2,1)}, u32[]{:S(2)}, u32[]{:S(2)}) collective-permute-start(bf16[96,768]{1,0:T(8,128)(2,1)S(1)} %pad_maximum_fusion.1.rest_0_), channel_id=1, source_target_pairs={{0,16},{1,17},{2,18},{3,19},{4,20},{5,21},{6,22},{7,23},{8,24},{9,... | collective-permute-start | bytes 442376 | tf_op jit(solution)/shard_map/ppermute | solution.py:579
  52.4 6.9 %copy-start.7 = (bf16[192,768]{1,0:T(8,128)(2,1)}, bf16[192,768]{1,0:T(8,128)(2,1)S(1)}, u32[]{:S(2)}) copy-start(bf16[192,768]{1,0:T(8,128)(2,1)S(1)} %collective-permute-done.17.qg1) | copy-start | bytes 884740
  52.4 11.3 %collective-permute-start.16 = (bf16[96,768]{1,0:T(8,128)(2,1)S(1)}, bf16[96,768]{1,0:T(8,128)(2,1)S(1)}, u32[]{:S(2)}, u32[]{:S(2)}) collective-permute-start(bf16[96,768]{1,0:T(8,128)(2,1)S(1)} %pad_maximum_fusion.1.rest_0_), channel_id=1, source_target_pairs={{0,24},{1,25},{2,26},{3,27},{4,28},{5,29},{6,30},{7,31},{8,16},{9,... | collective-permute-start | bytes 442376 | tf_op jit(solution)/shard_map/ppermute | solution.py:579
  54.1 5.1 %copy-start.8 = (bf16[192,768]{1,0:T(8,128)(2,1)}, bf16[192,768]{1,0:T(8,128)(2,1)S(1)}, u32[]{:S(2)}) copy-start(bf16[192,768]{1,0:T(8,128)(2,1)S(1)} %collective-permute-done.18.qg2) | copy-start | bytes 884740
  54.2 10.4 %collective-permute-start.19 = (bf16[192,768]{1,0:T(8,128)(2,1)S(1)}, bf16[192,768]{1,0:T(8,128)(2,1)S(1)}, u32[]{:S(2)}, u32[]{:S(2)}) collective-permute-start(bf16[192,768]{1,0:T(8,128)(2,1)S(1)} %collective-permute-done.18.qg2), channel_id=1, source_target_pairs={{0,1},{1,0},{2,3},{3,2},{4,5},{5,4},{6,7},{7,6},{8,9},{9,8},{10,11... | collective-permute-start | bytes 884744 | tf_op jit(solution)/shard_map/ppermute | solution.py:579
  63.0 10.8 %copy-start.20 = (f32[32,128]{1,0:T(8,128)S(1)}, f32[32,128]{1,0:T(8,128)}, u32[]{:S(2)}) copy-start(f32[32,128]{1,0:T(8,128)} %get-tuple-element.97.near_stat.st0) | copy-start | bytes 49156
  63.0 10.3 %collective-permute-start.20 = (f32[32,128]{1,0:T(8,128)}, f32[32,128]{1,0:T(8,128)S(1)}, u32[]{:S(2)}, u32[]{:S(2)}) collective-permute-start(f32[32,128]{1,0:T(8,128)} %get-tuple-element.97.near_stat.st0), channel_id=1, source_target_pairs={{0,1},{1,0},{2,3},{3,2},{4,5},{5,4},{6,7},{7,6},{8,9},{9,8},{10,11... | collective-permute-start | bytes 49160 | tf_op jit(solution)/shard_map/ppermute | solution.py:579
  63.1 24.7 %copy-start.10 = (bf16[96,768]{1,0:T(8,128)(2,1)}, bf16[96,768]{1,0:T(8,128)(2,1)S(1)}, u32[]{:S(2)}) copy-start(bf16[96,768]{1,0:T(8,128)(2,1)S(1)} %collective-permute-done.14.rest_1_) | copy-start | bytes 442372
  63.1 10.7 %collective-permute-start.21 = (f32[32,128]{1,0:T(8,128)}, f32[32,128]{1,0:T(8,128)S(1)}, u32[]{:S(2)}, u32[]{:S(2)}) collective-permute-start(f32[32,128]{1,0:T(8,128)} %get-tuple-element.97.near_stat.st0), channel_id=1, source_target_pairs={{0,2},{1,3},{2,0},{3,1},{4,6},{5,7},{6,4},{7,5},{8,10},{9,11},{10,... | collective-permute-start | bytes 49160 | tf_op jit(solution)/shard_map/ppermute | solution.py:579
  63.7 24.2 %collective-permute-start.23 = (bf16[96,768]{1,0:T(8,128)(2,1)S(1)}, bf16[96,768]{1,0:T(8,128)(2,1)S(1)}, u32[]{:S(2)}, u32[]{:S(2)}) collective-permute-start(bf16[96,768]{1,0:T(8,128)(2,1)S(1)} %pad_maximum_fusion.1.rest_0_), channel_id=1, source_target_pairs={{0,1},{1,0},{2,3},{3,2},{4,5},{5,4},{6,7},{7,6},{8,9},{9,8},{10,11... | collective-permute-start | bytes 442376 | tf_op jit(solution)/shard_map/ppermute | solution.py:579
  64.5 23.4 %collective-permute-start.24 = (bf16[96,768]{1,0:T(8,128)(2,1)S(1)}, bf16[96,768]{1,0:T(8,128)(2,1)S(1)}, u32[]{:S(2)}, u32[]{:S(2)}) collective-permute-start(bf16[96,768]{1,0:T(8,128)(2,1)S(1)} %collective-permute-done.14.rest_1_), channel_id=1, source_target_pairs={{0,1},{1,0},{2,3},{3,2},{4,5},{5,4},{6,7},{7,6},{8,9},{9,8},{10,11... | collective-permute-start | bytes 442376 | tf_op jit(solution)/shard_map/ppermute | solution.py:579
  64.6 10.6 %copy-start.9 = (bf16[192,768]{1,0:T(8,128)(2,1)}, bf16[192,768]{1,0:T(8,128)(2,1)S(1)}, u32[]{:S(2)}) copy-start(bf16[192,768]{1,0:T(8,128)(2,1)S(1)} %collective-permute-done.19.qg3) | copy-start | bytes 884740
  64.6 23.3 %collective-permute-start.25 = (bf16[96,768]{1,0:T(8,128)(2,1)}, bf16[96,768]{1,0:T(8,128)(2,1)S(1)}, u32[]{:S(2)}, u32[]{:S(2)}) collective-permute-start(bf16[96,768]{1,0:T(8,128)(2,1)} %collective-permute-done.15.rest_2_), channel_id=1, source_target_pairs={{0,1},{1,0},{2,3},{3,2},{4,5},{5,4},{6,7},{7,6},{8,9},{9,8},{10,11... | collective-permute-start | bytes 442376 | tf_op jit(solution)/shard_map/ppermute | solution.py:579
  65.1 8.2 %copy-start.12 = (bf16[96,768]{1,0:T(8,128)(2,1)S(1)}, bf16[96,768]{1,0:T(8,128)(2,1)}, u32[]{:S(2)}) copy-start(bf16[96,768]{1,0:T(8,128)(2,1)} %copy-done.11) | copy-start | bytes 442372
  65.1 23.4 %all-to-all-start.1 = ((bf16[64,8,768]{2,1,0:T(8,128)(2,1)}), bf16[64,8,768]{2,1,0:T(8,128)(2,1)}, u32[]{:S(2)}, u32[]{:S(2)}) async-start(bf16[64,8,768]{2,1,0:T(8,128)(2,1)} %bitcast.6), calls=%async_computation.1 | async-start | bytes 1572864 | tf_op jit(solution)/shard_map/all_to_all | solution.py:583
  73.3 14.5 %copy-start.21 = (f32[32,128]{1,0:T(8,128)}, f32[32,128]{1,0:T(8,128)S(1)}, u32[]{:S(2)}) copy-start(f32[32,128]{1,0:T(8,128)S(1)} %collective-permute-done.20.st1) | copy-start | bytes 49156
  73.3 14.6 %collective-permute-start.26 = (bf16[96,768]{1,0:T(8,128)(2,1)S(1)}, bf16[96,768]{1,0:T(8,128)(2,1)}, u32[]{:S(2)}, u32[]{:S(2)}) collective-permute-start(bf16[96,768]{1,0:T(8,128)(2,1)S(1)} %copy-done.12), channel_id=1, source_target_pairs={{0,1},{1,0},{2,3},{3,2},{4,5},{5,4},{6,7},{7,6},{8,9},{9,8},{10,11... | collective-permute-start | bytes 442376 | tf_op jit(solution)/shard_map/ppermute | solution.py:579
  73.8 14.1 %copy-start.22 = (f32[32,128]{1,0:T(8,128)}, f32[32,128]{1,0:T(8,128)S(1)}, u32[]{:S(2)}) copy-start(f32[32,128]{1,0:T(8,128)S(1)} %collective-permute-done.21.st2) | copy-start | bytes 49156
  73.8 14.1 %collective-permute-start.22 = (f32[32,128]{1,0:T(8,128)S(1)}, f32[32,128]{1,0:T(8,128)S(1)}, u32[]{:S(2)}, u32[]{:S(2)}) collective-permute-start(f32[32,128]{1,0:T(8,128)S(1)} %copy-done.20), channel_id=1, source_target_pairs={{0,3},{1,2},{2,1},{3,0},{4,7},{5,6},{6,5},{7,4},{8,11},{9,10},{10,... | collective-permute-start | bytes 49160 | tf_op jit(solution)/shard_map/ppermute | solution.py:579
  87.8 2.3 %copy-start.23 = (f32[32,128]{1,0:T(8,128)}, f32[32,128]{1,0:T(8,128)S(1)}, u32[]{:S(2)}) copy-start(f32[32,128]{1,0:T(8,128)S(1)} %collective-permute-done.22.st3) | copy-start | bytes 49156
  87.9 7.2 %copy-start.17 = (bf16[96,768]{1,0:T(8,128)(2,1)}, bf16[96,768]{1,0:T(8,128)(2,1)S(1)}, u32[]{:S(2)}) copy-start(bf16[96,768]{1,0:T(8,128)(2,1)S(1)} %collective-permute-done.23.rest_4_) | copy-start | bytes 442372
  87.9 2.2 %copy-start.18 = (bf16[96,768]{1,0:T(8,128)(2,1)}, bf16[96,768]{1,0:T(8,128)(2,1)S(1)}, u32[]{:S(2)}) copy-start(bf16[96,768]{1,0:T(8,128)(2,1)S(1)} %collective-permute-done.24.rest_5_) | copy-start | bytes 442372
  87.9 2.2 %copy-start.19 = (bf16[96,768]{1,0:T(8,128)(2,1)}, bf16[96,768]{1,0:T(8,128)(2,1)S(1)}, u32[]{:S(2)}) copy-start(bf16[96,768]{1,0:T(8,128)(2,1)S(1)} %collective-permute-done.25.rest_6_) | copy-start | bytes 442372
  88.5 6.6 %collective-permute-start.27 = (bf16[512,768]{1,0:T(8,128)(2,1)}, bf16[512,768]{1,0:T(8,128)(2,1)}, u32[]{:S(2)}, u32[]{:S(2)}) collective-permute-start(bf16[512,768]{1,0:T(8,128)(2,1)} %bitcast.4.far_a), channel_id=1, source_target_pairs={{0,1},{1,0},{2,3},{3,2},{4,5},{5,4},{6,7},{7,6},{8,9},{9,8},{10,11... | collective-permute-start | bytes 2359304 | tf_op jit(solution)/shard_map/ppermute | solution.py:579
  90.1 4.9 %copy-start = (s32[3,12]{1,0:T(4,128)S(1)}, s32[3,12]{1,0:T(4,128)}, u32[]{:S(2)}) copy-start(s32[3,12]{1,0:T(4,128)} %off.7) | copy-start | bytes 436
  (6 other events, 5.1 us)
where the time goes:
time: 104 us
  starting transfers between devices  46.8 us (45%)
  Pallas kernels  46.5 us (45%)
  waiting for transfers between devices  6.98 us (7%)
  local copies, waits for them, and re-layouts  2.41 us (2%)
  between operations  1.27 us (1%)
    pallas_call x9, Pallas kernels, run(): return kernel(*placed)  46.5 us
    ppermute x28, starting transfers between devices, flip(): return lax.ppermute(value, 'seq', pairs)  26.3 us
    all_to_all x2, starting transfers between devices, exchange(): lax.all_to_all(value, 'seq', 0, 0, tiled=True, axis_index_groups=groups)  20.5 us
    ppermute x28, waiting for transfers between devices, flip(): return lax.ppermute(value, 'seq', pairs)  6.43 us
    unnamed x48, local copies, waits for them, and re-layouts  2.38 us
  transfers between devices with their start and end apart: 30, of which 4 were waited for; matrix products, arithmetic and copies ran while one was open for 0% of the time, Pallas kernels for 32%

commit v1 on v0

--- a/solution.py
+++ b/solution.py
@@ -97,20 +97,26 @@
     )
 
 
-def head_lanes():
-    return iota((HEADS, 1, WIDTH), 2) >> 6 == iota((HEADS, 1, WIDTH), 0)
+def heads_of(slots):
+    return 16 if slots == 8 else HEADS
+
+
+def head_lanes(heads):
+    return iota((heads, 1, WIDTH), 2) >> 6 == iota((heads, 1, WIDTH), 0)
 
 
 def head_block(x, slots):
-    return jnp.where(head_lanes(), x[None], 0.0).reshape(HEADS * slots, WIDTH).astype(BF16)
+    heads = heads_of(slots)
+    return jnp.where(head_lanes(heads), x[None], 0.0).reshape(heads * slots, WIDTH).astype(BF16)
 
 
 def head_sum(x, slots):
-    return jnp.sum(jnp.where(head_lanes(), x.reshape(HEADS, slots, WIDTH), 0.0), axis=0)
+    heads = heads_of(slots)
+    return jnp.sum(jnp.where(head_lanes(heads), x.reshape(heads, slots, WIDTH), 0.0), axis=0)
 
 
 def stat_up(rows, slots, shift):
-    count = HEADS * slots
+    count = heads_of(slots) * slots
     bits = slots.bit_length() - 1
     own = iota((16, count), 1) >> bits == iota((16, count), 0)
     wide = jnp.concatenate([jnp.where(own, r, 0.0) for r in rows], axis=0)
@@ -120,7 +126,7 @@
 
 
 def stat_down(xs, slots, shift):
-    count = HEADS * slots
+    count = heads_of(slots) * slots
     bits = slots.bit_length() - 1
     down = one_hot(iota((TOK, count), 0) >> shift == (iota((TOK, count), 1) & (slots - 1)))
     wide = exact_nn(jnp.concatenate(xs, axis=0), down)
@@ -323,34 +329,29 @@
             total[2 * p + e : 2 * p + e + 1, :] = t[:, cols]
 
 
-def far_forward(kv, query, slots, slot_rows, count):
-    s = SCALE * nt(kv, head_block(query, slots))
-    s = jnp.where(in_slots(s.shape[0], slot_rows, 0, count, s.shape[1]), s, NEGATIVE)
+def softmax_parts(s):
     m = jnp.max(s, axis=0, keepdims=True)
     w = jnp.exp(s - m)
-    t = jnp.sum(w, axis=0, keepdims=True)
-    o = tn(pltpu.roll(w, count, 0).astype(BF16), kv)
-    return m, t, head_sum(o, slots)
+    return m, w, jnp.sum(w, axis=0, keepdims=True)
+
+
+def stack(refs, part):
+    return jnp.concatenate([r[part * 48 : part * 48 + 48, :] for r in refs], axis=0)
 
 
 def mid_forward_body(own, *rest):
     mids, (out2, peak2, total2) = rest[:8], rest[8:]
-    m, t, o = far_forward(stack(mids), own[32:48, :].astype(F32), 16, MID_SLOT, MID)
-    out2[...] = o
-    peak2[...] = m
-    total2[...] = t
+    s = SCALE * nt(stack(mids, 0), head_block(own[32:48, :].astype(F32), 16))
+    peak2[...], w, total2[...] = softmax_parts(s)
+    out2[...] = head_sum(tn(w.astype(BF16), stack(mids, 1)), 16)
 
 
 def far_forward_body(far_a, far_b, own, out3, peak3, total3):
     far = jnp.concatenate([far_a[...], far_b[...]], axis=0)
-    m, t, o = far_forward(far, own[96:112, :].astype(F32)[0:8], 8, FAR_SLOT, FAR)
-    out3[...] = o
-    peak3[...] = m
-    total3[...] = t
-
-
-def stack(refs):
-    return jnp.concatenate([r[...] for r in refs], axis=0)
+    s = SCALE * nt(far, head_block(own[96:112, :].astype(F32)[0:8], 8))
+    s = jnp.where(in_slots(s.shape[0], FAR_SLOT, 0, FAR, s.shape[1]), s, NEGATIVE)
+    peak3[...], w, total3[...] = softmax_parts(s)
+    out3[...] = head_sum(tn(pltpu.roll(w, FAR, 0).astype(BF16), far), 8)
 
 
 def merge_body(
@@ -422,14 +423,23 @@
         far_send[d * 16 : (d + 1) * 16, :] = send
 
 
-def far_query_grad(kv, query, grad, lse, delta, slots, slot_rows, count):
-    s = SCALE * nt(kv, head_block(query, slots))
-    valid = in_slots(s.shape[0], slot_rows, 0, count, s.shape[1])
+def far_products(rows, first, second):
+    both = nt(rows, jnp.concatenate([head_block(first, 8), head_block(second, 8)], axis=0))
+    return SCALE * both[:, 0:128], pltpu.roll(both[:, 128:256], rows.shape[0] - FAR, 0)
+
+
+def far_query_grad(kv, query, grad, lse, delta):
+    s, dp = far_products(kv, query, grad)
+    valid = in_slots(s.shape[0], FAR_SLOT, 0, FAR, s.shape[1])
     prob = jnp.exp(jnp.where(valid, s - lse, NEGATIVE))
-    dp = nt(kv, head_block(grad, slots))
-    dp = pltpu.roll(dp, dp.shape[0] - count, 0)
     ds = jnp.where(valid, prob * (dp - delta), 0.0).astype(BF16)
-    return SCALE * head_sum(tn(ds, kv), slots)
+    return SCALE * head_sum(tn(ds, kv), 8)
+
+
+def mid_query_grad(keys, values, query, grad, lse, delta):
+    prob = jnp.exp(SCALE * nt(keys, head_block(query, 16)) - lse)
+    ds = (prob * (nt(values, head_block(grad, 16)) - delta)).astype(BF16)
+    return SCALE * head_sum(tn(ds, keys), 16)
 
 
 def local_grad_body(
@@ -457,13 +467,12 @@
     down = []
     for b, slots in ((1, 16), (2, 8)):
         down += stat_down([jnp.where(taken[b], x[...], 0.0) for x in (lse, delta)], slots, SHIFTS[b])
-    dq2 = far_query_grad(
-        stack(mids), own[32:48, :].astype(F32), own[48:64, :].astype(F32),
-        down[0], down[1], 16, MID_SLOT, MID,
+    dq2 = mid_query_grad(
+        stack(mids, 0), stack(mids, 1), own[32:48, :].astype(F32), own[48:64, :].astype(F32),
+        down[0], down[1],
     )
     dq3 = far_query_grad(
-        far, own[96:112, :].astype(F32)[0:8], own[112:128, :].astype(F32)[0:8],
-        down[2], down[3], 8, FAR_SLOT, FAR,
+        far, own[96:112, :].astype(F32)[0:8], own[112:128, :].astype(F32)[0:8], down[2], down[3]
     )
     s1 = spread_near_t(near_t[...])
     s2 = spread_t(dq2, 16, SHIFTS[1])
@@ -491,55 +500,55 @@
         grad_q[:, lanes] = jnp.concatenate(parts, axis=0).T.astype(BF16)
 
 
-def near_key_body(
-    kv, qg0, qg1, qg2, qg3, st0, st1, st2, st3, dk_near, dv_near
-):
+def near_key_body(kv, qg0, qg1, qg2, qg3, st0, st1, st2, st3, dk_near, dv_near):
+    refs = (qg0, qg1, qg2, qg3)
+    stats = jnp.concatenate([st[:, 0:NEAR] for st in (st0, st1, st2, st3)], axis=1)
+    head = iota((2 * NEAR, TOK), 0) < NEAR
+    first = iota((NEAR, LANES), 1) < HEAD_DIM
     for p in range(PAIRS):
         lanes = slice(p * LANES, (p + 1) * LANES)
-        kb = pair_block(kv[0:NEAR, lanes])
-        vb = pair_block(kv[NEAR : 2 * NEAR, lanes])
-        head = iota((2 * NEAR, NEAR), 0) < NEAR
-        dk = jnp.zeros((2 * NEAR, LANES), F32)
-        dv = jnp.zeros((2 * NEAR, LANES), F32)
-        for qg, st in ((qg0, st0), (qg1, st1), (qg2, st2), (qg3, st3)):
-            h = 2 * p
-            queries = qg[0:NEAR, lanes]
-            grads = qg[NEAR : 2 * NEAR, lanes]
-            lr = jnp.where(head, st[h : h + 1, 0:NEAR], st[h + 1 : h + 2, 0:NEAR])
-            dr = jnp.where(head, st[16 + h : 17 + h, 0:NEAR], st[17 + h : 18 + h, 0:NEAR])
-            prob = jnp.exp(SCALE * nt(kb, queries) - lr)
-            ds = (prob * (nt(vb, grads) - dr)).astype(BF16)
-            dk = dk + nn(ds, queries)
-            dv = dv + nn(prob.astype(BF16), grads)
-        first = iota((NEAR, LANES), 1) < HEAD_DIM
+        h = 2 * p
+        queries = near_pair(refs, 0, lanes)
+        grads = near_pair(refs, 1, lanes)
+        lr = jnp.where(head, stats[h : h + 1], stats[h + 1 : h + 2])
+        dr = jnp.where(head, stats[16 + h : 17 + h], stats[17 + h : 18 + h])
+        prob = jnp.exp(SCALE * nt(pair_block(kv[0:NEAR, lanes]), queries) - lr)
+        ds = (prob * (nt(pair_block(kv[NEAR : 2 * NEAR, lanes]), grads) - dr)).astype(BF16)
+        dk = nn(ds, queries)
+        dv = nn(prob.astype(BF16), grads)
         dk_near[:, lanes] = SCALE * jnp.where(first, dk[0:NEAR], dk[NEAR:])
         dv_near[:, lanes] = jnp.where(first, dv[0:NEAR], dv[NEAR:])
 
 
-def stat_expand(line, slot_rows, first, low, count, slots):
-    devices = line.shape[0]
-    slot = iota((1, slot_rows, WIDTH), 1) - low
-    mask = ((iota((1, slot_rows, WIDTH), 2) & 15) == slot + first) & (slot >= 0) & (slot < count)
-    x = jnp.where(mask, line[:, None, :], 0.0).reshape(devices * slot_rows, WIDTH).astype(BF16)
-    columns = HEADS * slots
+def stat_pick(slots):
+    columns = heads_of(slots) * slots
     bits = slots.bit_length() - 1
-    pick = one_hot(
+    return one_hot(
         (iota((WIDTH, columns), 0) & 255) >> 4 == iota((WIDTH, columns), 1) >> bits
     )
-    return nn(x, pick)
-
-
-def far_key_grad(qg, key, value, lse, delta, slots, slot_rows, count):
-    rows = qg.shape[0]
-    s = SCALE * nt(qg, head_block(key, slots))
-    valid = in_slots(rows, slot_rows, 0, count, s.shape[1])
+
+
+def far_expand(line, pick):
+    slot = iota((1, FAR_SLOT, WIDTH), 1)
+    mask = ((iota((1, FAR_SLOT, WIDTH), 2) & 15) == slot + MID) & (slot < FAR)
+    x = jnp.where(mask, line[:, None, :], 0.0).reshape(line.shape[0] * FAR_SLOT, WIDTH)
+    return nn(x.astype(BF16), pick)
+
+
+def far_key_grad(qg, key, value, lse, delta):
+    s, dp = far_products(qg, key, value)
+    valid = in_slots(s.shape[0], FAR_SLOT, 0, FAR, s.shape[1])
     prob = jnp.exp(jnp.where(valid, s - lse, NEGATIVE))
-    dp = nt(qg, head_block(value, slots))
-    dp = pltpu.roll(dp, rows - count, 0)
     ds = jnp.where(valid, prob * (dp - delta), 0.0).astype(BF16)
-    dk = SCALE * head_sum(tn(ds, qg), slots)
-    dv = head_sum(tn(pltpu.roll(prob, count, 0).astype(BF16), qg), slots)
+    dk = SCALE * head_sum(tn(ds, qg), 8)
+    dv = head_sum(tn(pltpu.roll(prob, FAR, 0).astype(BF16), qg), 8)
     return dk, dv
+
+
+def mid_key_grad(queries, grads, key, value, lse, delta):
+    prob = jnp.exp(SCALE * nt(queries, head_block(key, 16)) - lse)
+    ds = (prob * (nt(grads, head_block(value, 16)) - delta)).astype(BF16)
+    return SCALE * head_sum(tn(ds, queries), 16), head_sum(tn(prob.astype(BF16), grads), 16)
 
 
 def key_grad_body(off, place, dk0, dv0, dk1, dv1, far_a, far_b, own, *rest):
@@ -551,12 +560,22 @@
     source = ((line >> 4) & 1) * (CHIPS * FAR_SLOT) + chip * FAR_SLOT + 6 + (line >> 5)
     lines2 = nn(one_hot(iota(line.shape, 1) == source), far)
     lines3 = far.astype(F32).reshape(2 * CHIPS, FAR_SLOT, WIDTH)
-    lse2 = stat_expand(lines2[0:32], MID_SLOT, 0, 0, MID, 16)
-    delta2 = stat_expand(lines2[32:64], MID_SLOT, 0, 0, MID, 16)
-    dk2, dv2 = far_key_grad(stack(mids), own32[0:16], own32[16:32], lse2, delta2, 16, MID_SLOT, MID)
-    lse3 = stat_expand(lines3[:, 6, :], FAR_SLOT, MID, 0, FAR, 8)
-    delta3 = stat_expand(lines3[:, 7, :], FAR_SLOT, MID, 0, FAR, 8)
-    dk3, dv3 = far_key_grad(far, own32[64:72], own32[80:88], lse3, delta3, 8, FAR_SLOT, FAR)
+    device = iota((TOK, 32), 1) * MID
+    row = iota((TOK, 32), 0)
+    spread = one_hot((row >= device) & (row < device + MID))
+    slot = lax.rem(iota((TOK, 1), 0), MID)
+    mask = (iota((TOK, WIDTH), 1) & 15) == slot
+    lines2 = lines2.astype(BF16)
+    pick2 = stat_pick(16)
+    lse2, delta2 = (
+        nn(jnp.where(mask, nn(spread, lines2[32 * e : 32 * e + 32]), 0.0).astype(BF16), pick2)
+        for e in range(2)
+    )
+    dk2, dv2 = mid_key_grad(stack(mids, 0), stack(mids, 1), own32[0:16], own32[16:32], lse2, delta2)
+    pick3 = stat_pick(8)
+    lse3 = far_expand(lines3[:, 6, :], pick3)
+    delta3 = far_expand(lines3[:, 7, :], pick3)
+    dk3, dv3 = far_key_grad(far, own32[64:72], own32[80:88], lse3, delta3)
     token = iota((TOK, WIDTH), 0)
     taken = [(token & (SPANS[b] - 1)) == offset_row(off, b) for b in range(3)]
     outs = []
@@ -644,8 +663,11 @@
     far_a = exchange(far_rep, chip_groups)
     lines = [mid_kvqg] + [flip(mid_kvqg, d) for d in (2, 4, 6)]
     near_kvs = near_gather(near_kv)
-    mid_kv = jnp.concatenate([x[:MID_SLOT] for x in lines], axis=0)
-    mid_qg = jnp.concatenate([x[MID_SLOT:] for x in lines], axis=0)
+    parts = [
+        jnp.concatenate([x[a * MID : (a + 1) * MID] for x in lines], axis=0) for a in range(4)
+    ]
+    mid_kv = jnp.concatenate(parts[0:2], axis=0)
+    mid_qg = jnp.concatenate(parts[2:4], axis=0)
     mid_kvs = plane_row(mid_kv)
 
     out0, peak0, total0 = call(
@@ -667,12 +689,11 @@
         held=(0, 1, 2, 3, 4),
         kept_out=(0, 1, 2),
     )(after((near_qg,), peak0)[0], *near_kvs)
-    near_qgs = near_first(after((near_qg,), peak0)[0])
-    mid_kvs = after(mid_kvs, peak1)
+    near_qgs = near_first(after((near_qg,), mid_kv)[0])
+    mid_kvs, near_qgs = after((tuple(mid_kvs), near_qgs), peak1)
     far_a = after((far_a,), *mid_kvs)[0]
     far_b = flip(far_a, 1)
-    near_qgs = near_second(after(near_qgs, far_a))
-    mid_qgs = plane_row(after((mid_qg,), far_a)[0])
+    near_qgs = near_second(near_qgs)
     mid_kvs = list(mid_kvs) + [flip(x, 1) for x in mid_kvs]
     out2, peak2, total2 = call(
         mid_forward_body,
@@ -685,7 +706,7 @@
     )(own, *mid_kvs)
     out3, peak3, total3 = call(
         far_forward_body,
-        [shape(8, WIDTH, F32), shape(1, 96, F32), shape(1, 96, F32)],
+        [shape(8, WIDTH, F32), shape(1, 128, F32), shape(1, 128, F32)],
         (),
         3,
         (),
@@ -714,9 +735,8 @@
 
     back_a = exchange(far_send, chip_groups)
     near_stats = near_direct(near_stat)
-    mid_qgs = after(mid_qgs, lse)
-    near_qg = after((near_qg,), lse, *mid_qgs, *near_qgs)[0]
-    mid_qgs = list(mid_qgs) + [flip(x, 1) for x in mid_qgs]
+    mid_qgs = plane_row(after((mid_qg,), lse)[0])
+    near_qg = after((near_qg,), lse, *near_qgs)[0]
 
     grad_q, dk0, dv0 = call(
         local_grad_body,
@@ -739,7 +759,9 @@
         offsets, queries, keys, values, grad_out, near_qg, *near_kvs, far_a, far_b, own, lse,
         delta, near_stat, *mid_kvs,
     )
-    back_a = after((back_a,), grad_q, *near_stats, *mid_qgs)[0]
+    mid_qgs = after(mid_qgs, grad_q)
+    back_a = after((back_a,), *mid_qgs, *near_stats)[0]
+    mid_qgs = list(mid_qgs) + [flip(x, 1) for x in mid_qgs]
     back_b = flip(back_a, 1)
     dk1, dv1 = call(
         near_key_body,

time: 104 us -> 100 us (0.962)
  Pallas kernels: 46.5 us -> 44 us
  waiting for transfers between devices: 6.98 us -> 5.61 us
    pallas_call x9, Pallas kernels: 46.5 us -> 44 us  [run(): return kernel(*placed)]
    ppermute x28, waiting for transfers between devices: 6.43 us -> 4.85 us  [flip(): return lax.ppermute(value, 'seq', pairs)]
    concatenate x0 -> x2, local copies, waits for them, and re-layouts: none -> 1.12 us  [the longest x1 0.58 us: on_device(): mid_kv = jnp.concatenate(parts[0:2], axis=0)]
    unnamed x48 -> x38, local copies, waits for them, and re-layouts: 2.38 us -> 1.46 us
  transfers between devices with their start and end apart: 30 -> 30, of which waited for: 4 -> 5; matrix products, arithmetic and copies ran while one was open for 0% -> 1% of each run, Pallas kernels for 32% -> 31%
where the time goes in v1:
time: 100 us; the launch traced here: 99.5 us
  starting transfers between devices  46 us (46%)
  Pallas kernels  44 us (44%)
  waiting for transfers between devices  5.61 us (6%)
  local copies, waits for them, and re-layouts  2.64 us (3%)
  between operations  1.22 us (1%)
    pallas_call x9, Pallas kernels, run(): return kernel(*placed)  44 us
    ppermute x28, starting transfers between devices, flip(): return lax.ppermute(value, 'seq', pairs)  25.5 us
    all_to_all x2, starting transfers between devices, exchange(): lax.all_to_all(value, 'seq', 0, 0, tiled=True, axis_index_groups=groups)  20.5 us
    ppermute x28, waiting for transfers between devices, flip(): return lax.ppermute(value, 'seq', pairs)  4.85 us
  transfers between devices with their start and end apart: 30, of which 5 were waited for; matrix products, arithmetic and copies ran while one was open for 1% of the time, Pallas kernels for 31%

profile of v1, /device:TPU:1, one launch (start us, length us, event | category | flops | bytes accessed | tf_op | source)
XLA Modules:
  0.0 99.5 jit_solution(8113495145235577212)
XLA Ops:
  0.6 4.3 %shard_map.84 = (bf16[192,768]{1,0:T(8,128)(2,1)}, bf16[192,768]{1,0:T(8,128)(2,1)}, bf16[48,768]{1,0:T(8,128)(2,1)}, bf16[512,768]{1,0:T(8,128)(2,1)}, bf16[16,...) custom-call(s32[3,12]{1,0:T(4,128)} %off.7, ...), custom_call_target="tpu_custom_call" | custom-call | flops 5000000000 | bytes 15000000 | tf_op jit(solution)/shard_map/pallas_call | solution.py:201
  5.0 3.6 %collective-permute-start.2 = (bf16[48,768]{1,0:T(8,128)(2,1)}, bf16[48,768]{1,0:T(8,128)(2,1)S(1)}, u32[]{:S(2)}, u32[]{:S(2)}) collective-permute-start(bf16[48,768]{1,0:T(8,128)(2,1)} %get-tuple-element.59), channel_id=1, source_target_pairs={{0,6},{1,7},{2,4},{3,5},{4,2},{5,3},{6,0},{7,1},{8,14},{9,15},{10,... | collective-permute-start | bytes 221192 | tf_op jit(solution)/shard_map/ppermute | solution.py:598
  8.6 0.3 collective-permute-start.1
  9.0 0.3 collective-permute-start
  9.3 1.1 %collective-permute-start.4 = (bf16[192,768]{1,0:T(8,128)(2,1)}, bf16[192,768]{1,0:T(8,128)(2,1)S(1)}, u32[]{:S(2)}, u32[]{:S(2)}) collective-permute-start(bf16[192,768]{1,0:T(8,128)(2,1)} %get-tuple-element.105.kv0.kv), channel_id=1, source_target_pairs={{0,2},{1,3},{2,0},{3,1},{4,6},{5,7},{6,4},{7,5},{8,10},{9,11},{10,... | collective-permute-start | bytes 884744 | tf_op jit(solution)/shard_map/ppermute | solution.py:598
  10.4 1.8 %collective-permute-start.3 = (bf16[192,768]{1,0:T(8,128)(2,1)}, bf16[192,768]{1,0:T(8,128)(2,1)S(1)}, u32[]{:S(2)}, u32[]{:S(2)}) collective-permute-start(bf16[192,768]{1,0:T(8,128)(2,1)} %get-tuple-element.105.kv0.kv), channel_id=1, source_target_pairs={{0,1},{1,0},{2,3},{3,2},{4,5},{5,4},{6,7},{7,6},{8,9},{9,8},{10,11... | collective-permute-start | bytes 884744 | tf_op jit(solution)/shard_map/ppermute | solution.py:598
  12.2 11.1 %all-to-all-start = ((bf16[64,8,768]{2,1,0:T(8,128)(2,1)}), bf16[64,8,768]{2,1,0:T(8,128)(2,1)}, u32[]{:S(2)}, u32[]{:S(2)}) async-start(bf16[64,8,768]{2,1,0:T(8,128)(2,1)} %bitcast.5), calls=%async_computation | async-start | bytes 1572864 | tf_op jit(solution)/shard_map/all_to_all | solution.py:602
  23.4 0.4 collective-permute-start.5
  23.8 0.6 concatenate.6.rest_0_
  24.4 2.5 %collective-permute-start.8 = (bf16[96,768]{1,0:T(8,128)(2,1)S(1)}, bf16[96,768]{1,0:T(8,128)(2,1)}, u32[]{:S(2)}, u32[]{:S(2)}) collective-permute-start(bf16[96,768]{1,0:T(8,128)(2,1)S(1)} %concatenate.6.rest_0_), channel_id=1, source_target_pairs={{0,24},{1,25},{2,26},{3,27},{4,28},{5,29},{6,30},{7,31},{8,16},{9,... | collective-permute-start | bytes 442376 | tf_op jit(solution)/shard_map/ppermute | solution.py:598
  27.0 0.6 collective-permute-start.7
  27.5 0.2 collective-permute-start.6
  27.8 1.2 %collective-permute-start.10 = (bf16[192,768]{1,0:T(8,128)(2,1)}, bf16[192,768]{1,0:T(8,128)(2,1)}, u32[]{:S(2)}, u32[]{:S(2)}) collective-permute-start(bf16[192,768]{1,0:T(8,128)(2,1)} %get-tuple-element.92.qg.qg0), channel_id=1, source_target_pairs={{0,2},{1,3},{2,0},{3,1},{4,6},{5,7},{6,4},{7,5},{8,10},{9,11},{10,... | collective-permute-start | bytes 884744 | tf_op jit(solution)/shard_map/ppermute | solution.py:598
  29.0 1.1 %collective-permute-start.9 = (bf16[192,768]{1,0:T(8,128)(2,1)}, bf16[192,768]{1,0:T(8,128)(2,1)}, u32[]{:S(2)}, u32[]{:S(2)}) collective-permute-start(bf16[192,768]{1,0:T(8,128)(2,1)} %get-tuple-element.92.qg.qg0), channel_id=1, source_target_pairs={{0,1},{1,0},{2,3},{3,2},{4,5},{5,4},{6,7},{7,6},{8,9},{9,8},{10,11... | collective-permute-start | bytes 884744 | tf_op jit(solution)/shard_map/ppermute | solution.py:598
  30.2 3.4 %shard_map.85 = (f32[768,384]{1,0:T(8,128)S(1)}, f32[16,384]{1,0:T(8,128)S(1)}, f32[16,384]{1,0:T(8,128)S(1)}) custom-call(bf16[384,768]{1,0:T(8,128)(2,1)S(1)} %get-tuple-element.57.q, bf16[384,768]{1,0:T(8,128)(2,1)S(1)} %get-tuple-element.60.k, bf16[384,768]{1,0:T(8,128)(2,1)S(1)} %get-tuple-element.61.v), custom_call_target="tpu_custom_call" | custom-call | flops 5000000000 | bytes 15000000 | tf_op jit(solution)/shard_map/pallas_call | solution.py:201
  33.6 3.3 %shard_map.86 = (f32[768,128]{1,0:T(8,128)S(1)}, f32[16,128]{1,0:T(8,128)S(1)}, f32[16,128]{1,0:T(8,128)S(1)}) custom-call(bf16[192,768]{1,0:T(8,128)(2,1)} %get-tuple-element.92.qg.qg0, bf16[192,768]{1,0:T(8,128)(2,1)} %get-tuple-element.105.kv0.kv, bf16[192,768]{1,0:T(8,128)(2,1)} %copy-done.5, bf16[192,768]{1,0:T(8,128)(2,1)} %copy-done.4, ...), custom_call_target="tpu_custom_call" | custom-call | flops 1000000000 | bytes 3000000 | tf_op jit(solution)/shard_map/pallas_call | solution.py:201
  36.8 3.8 %collective-permute-done.8.rest_3_ = bf16[96,768]{1,0:T(8,128)(2,1)} collective-permute-done((bf16[96,768]{1,0:T(8,128)(2,1)S(1)}, bf16[96,768]{1,0:T(8,128)(2,1)}, u32[]{:S(2)}, u32[]{:S(2)}) %collective-permute-start.8) | collective-permute-done | bytes 147488 | tf_op jit(solution)/shard_map/ppermute | solution.py:598
  40.7 1.1 %collective-permute-start.15 = (bf16[512,768]{1,0:T(8,128)(2,1)}, bf16[512,768]{1,0:T(8,128)(2,1)}, u32[]{:S(2)}, u32[]{:S(2)}) collective-permute-start(bf16[512,768]{1,0:T(8,128)(2,1)} %bitcast.1.far_a), channel_id=1, source_target_pairs={{0,1},{1,0},{2,3},{3,2},{4,5},{5,4},{6,7},{7,6},{8,9},{9,8},{10,11... | collective-permute-start | bytes 2359304 | tf_op jit(solution)/shard_map/ppermute | solution.py:598
  41.8 0.1 collective-permute-start.11
  41.9 0.4 collective-permute-start.12
  42.3 0.1 collective-permute-start.13
  42.4 0.4 collective-permute-start.14
  42.8 0.5 concatenate.7.rest_0_
  43.3 0.7 collective-permute-done.11.rest_4_
  44.0 0.4 collective-permute-start.16
  44.4 0.1 collective-permute-done.13.rest_6_
  44.5 0.2 collective-permute-done.14.rest_7_
  44.7 0.3 copy-done.9
  45.0 0.1 copy-done.10
  45.2 0.2 copy-done.11
  45.4 2.4 %shard_map.87 = (f32[16,768]{1,0:T(8,128)S(1)}, f32[1,192]{1,0:T(1,128)S(1)}, f32[1,192]{1,0:T(1,128)S(1)}) custom-call(bf16[128,768]{1,0:T(8,128)(2,1)} %get-tuple-element.82.own, bf16[96,768]{1,0:T(8,128)(2,1)} %copy-done.2, bf16[96,768]{1,0:T(8,128)(2,1)} %collective-permute-done.6.rest_1_, bf16[96,768]{1,0:T(8,128)(2,1)} %collective-permute-done.7.rest_2_, ...), custom_call_target="tpu_custom_call" | custom-call | flops 5000000000 | bytes 15000000 | tf_op jit(solution)/shard_map/pallas_call | solution.py:201
  47.8 2.8 %shard_map.88 = (f32[8,768]{1,0:T(8,128)S(1)}, f32[1,128]{1,0:T(1,128)S(1)}, f32[1,128]{1,0:T(1,128)S(1)}) custom-call(bf16[512,768]{1,0:T(8,128)(2,1)} %bitcast.1.far_a, bf16[512,768]{1,0:T(8,128)(2,1)} %collective-permute-done.15.far_b, bf16[128,768]{1,0:T(8,128)(2,1)} %get-tuple-element.82.own), custom_call_target="tpu_custom_call" | custom-call | flops 5000000000 | bytes 15000000 | tf_op jit(solution)/shard_map/pallas_call | solution.py:201
  50.6 3.7 %shard_map.89 = (bf16[384,768]{1,0:T(8,128)(2,1)}, f32[16,384]{1,0:T(8,128)S(1)}, f32[16,384]{1,0:T(8,128)S(1)}, f32[32,128]{1,0:T(8,128)}, bf16[512,768]{1,0:T(8,128)(2,1)}) custom-call(s32[3,12]{1,0:T(4,128)} %off.7, bf16[384,768]{1,0:T(8,128)(2,1)} %g_hbm.1, f32[768,384]{1,0:T(8,128)S(1)} %get-tuple-element.62.out0, ...), custom_call_target="tpu_custom_call" | custom-call | flops 5000000000 | bytes 15000000 | tf_op jit(solution)/shard_map/pallas_call | solution.py:201
  54.3 1.1 %collective-permute-start.19 = (bf16[96,768]{1,0:T(8,128)(2,1)S(1)}, bf16[96,768]{1,0:T(8,128)(2,1)}, u32[]{:S(2)}, u32[]{:S(2)}) collective-permute-start(bf16[96,768]{1,0:T(8,128)(2,1)S(1)} %concatenate.7.rest_0_), channel_id=1, source_target_pairs={{0,24},{1,25},{2,26},{3,27},{4,28},{5,29},{6,30},{7,31},{8,16},{9,... | collective-permute-start | bytes 442376 | tf_op jit(solution)/shard_map/ppermute | solution.py:598
  55.4 1.2 %collective-permute-start.22 = (f32[32,128]{1,0:T(8,128)}, f32[32,128]{1,0:T(8,128)S(1)}, u32[]{:S(2)}, u32[]{:S(2)}) collective-permute-start(f32[32,128]{1,0:T(8,128)} %get-tuple-element.94.near_stat.st0), channel_id=1, source_target_pairs={{0,3},{1,2},{2,1},{3,0},{4,7},{5,6},{6,5},{7,4},{8,11},{9,10},{10,... | collective-permute-start | bytes 49160 | tf_op jit(solution)/shard_map/ppermute | solution.py:598
  56.6 0.8 collective-permute-start.21
  57.4 0.1 collective-permute-start.20
  57.6 0.7 collective-permute-start.18
  58.3 9.4 %all-to-all-start.1 = ((bf16[64,8,768]{2,1,0:T(8,128)(2,1)}), bf16[64,8,768]{2,1,0:T(8,128)(2,1)}, u32[]{:S(2)}, u32[]{:S(2)}) async-start(bf16[64,8,768]{2,1,0:T(8,128)(2,1)} %bitcast.6), calls=%async_computation.1 | async-start | bytes 1572864 | tf_op jit(solution)/shard_map/all_to_all | solution.py:602
  67.7 1.2 %collective-permute-start.17 = (bf16[96,768]{1,0:T(8,128)(2,1)S(1)}, bf16[96,768]{1,0:T(8,128)(2,1)}, u32[]{:S(2)}, u32[]{:S(2)}) collective-permute-start(bf16[96,768]{1,0:T(8,128)(2,1)S(1)} %concatenate.7.rest_0_), channel_id=1, source_target_pairs={{0,8},{1,9},{2,10},{3,11},{4,12},{5,13},{6,14},{7,15},{8,0},{9,1},... | collective-permute-start | bytes 442376 | tf_op jit(solution)/shard_map/ppermute | solution.py:598
  68.9 12.4 %shard_map.90 = (bf16[384,768]{1,0:T(8,128)(2,1)}, f32[2304,128]{1,0:T(8,128)S(1)}, f32[2304,128]{1,0:T(8,128)S(1)}) custom-call(s32[3,12]{1,0:T(4,128)} %off.7, bf16[384,768]{1,0:T(8,128)(2,1)} %q_hbm.1, bf16[384,768]{1,0:T(8,128)(2,1)} %k_hbm.1, bf16[384,768]{1,0:T(8,128)(2,1)} %v_hbm.1, bf16[384,768]{1,0:T(8,128)(2,1)} %g_hbm.1, ...), custom_call_target="tpu_custom_call" | custom-call | flops 10000000000 | bytes 30000000 | tf_op jit(solution)/shard_map/pallas_call | solution.py:201
  81.5 0.8 all-to-all-done.1
  82.2 3.5 %collective-permute-start.23 = (bf16[512,768]{1,0:T(8,128)(2,1)}, bf16[512,768]{1,0:T(8,128)(2,1)}, u32[]{:S(2)}, u32[]{:S(2)}) collective-permute-start(bf16[512,768]{1,0:T(8,128)(2,1)} %bitcast.4.far_a), channel_id=1, source_target_pairs={{0,1},{1,0},{2,3},{3,2},{4,5},{5,4},{6,7},{7,6},{8,9},{9,8},{10,11... | collective-permute-start | bytes 2359304 | tf_op jit(solution)/shard_map/ppermute | solution.py:598
  85.8 0.4 collective-permute-start.25
  86.3 0.4 collective-permute-start.27
  86.7 3.1 %shard_map.91 = (f32[96,768]{1,0:T(8,128)S(1)}, f32[96,768]{1,0:T(8,128)S(1)}) custom-call(bf16[192,768]{1,0:T(8,128)(2,1)} %get-tuple-element.105.kv0.kv, bf16[192,768]{1,0:T(8,128)(2,1)} %get-tuple-element.92.qg.qg0, bf16[192,768]{1,0:T(8,128)(2,1)} %collective-permute-done.9.qg1, bf16[192,768]{1,0:T(8,128)(2,1)} %collective-permute-done.10.qg2, ...), custom_call_target="tpu_custom_call" | custom-call | flops 5000000000 | bytes 15000000 | tf_op jit(solution)/shard_map/pallas_call | solution.py:201
  89.9 0.6 copy-done.12
  90.7 8.6 %shard_map.92 = (bf16[384,768]{1,0:T(8,128)(2,1)}, bf16[384,768]{1,0:T(8,128)(2,1)}) custom-call(s32[3,12]{1,0:T(4,128)S(1)} %copy-done, s32[1]{0:T(128)} %bitcast.2.place, f32[2304,128]{1,0:T(8,128)S(1)} %get-tuple-element.96.dk0, f32[2304,128]{1,0:T(8,128)S(1)} %get-tuple-element.97.dv0, f32[96,768]{1,0:T(8,128)S(1)} %get-tuple-element.106.dk1, ...), custom_call_target="tpu_custom_call" | custom-call | flops 5000000000 | bytes 15000000 | tf_op jit(solution)/shard_map/pallas_call | solution.py:201
  (65 shorter events, 0.5 us)
Async XLA Ops:
  5.0 18.4 %copy-start.3 = (bf16[48,768]{1,0:T(8,128)(2,1)S(1)}, bf16[48,768]{1,0:T(8,128)(2,1)}, u32[]{:S(2)}) copy-start(bf16[48,768]{1,0:T(8,128)(2,1)} %get-tuple-element.59) | copy-start | bytes 221188
  5.0 18.4 %collective-permute-start.2 = (bf16[48,768]{1,0:T(8,128)(2,1)}, bf16[48,768]{1,0:T(8,128)(2,1)S(1)}, u32[]{:S(2)}, u32[]{:S(2)}) collective-permute-start(bf16[48,768]{1,0:T(8,128)(2,1)} %get-tuple-element.59), channel_id=1, source_target_pairs={{0,6},{1,7},{2,4},{3,5},{4,2},{5,3},{6,0},{7,1},{8,14},{9,15},{10,... | collective-permute-start | bytes 221192 | tf_op jit(solution)/shard_map/ppermute | solution.py:598
  8.6 15.2 %collective-permute-start.1 = (bf16[48,768]{1,0:T(8,128)(2,1)}, bf16[48,768]{1,0:T(8,128)(2,1)S(1)}, u32[]{:S(2)}, u32[]{:S(2)}) collective-permute-start(bf16[48,768]{1,0:T(8,128)(2,1)} %get-tuple-element.59), channel_id=1, source_target_pairs={{0,4},{1,5},{2,6},{3,7},{4,0},{5,1},{6,2},{7,3},{8,12},{9,13},{10,... | collective-permute-start | bytes 221192 | tf_op jit(solution)/shard_map/ppermute | solution.py:598
  9.0 14.8 %collective-permute-start = (bf16[48,768]{1,0:T(8,128)(2,1)}, bf16[48,768]{1,0:T(8,128)(2,1)S(1)}, u32[]{:S(2)}, u32[]{:S(2)}) collective-permute-start(bf16[48,768]{1,0:T(8,128)(2,1)} %get-tuple-element.59), channel_id=1, source_target_pairs={{0,2},{1,3},{2,0},{3,1},{4,6},{5,7},{6,4},{7,5},{8,10},{9,11},{10,... | collective-permute-start | bytes 221192 | tf_op jit(solution)/shard_map/ppermute | solution.py:598
  9.3 14.1 %collective-permute-start.4 = (bf16[192,768]{1,0:T(8,128)(2,1)}, bf16[192,768]{1,0:T(8,128)(2,1)S(1)}, u32[]{:S(2)}, u32[]{:S(2)}) collective-permute-start(bf16[192,768]{1,0:T(8,128)(2,1)} %get-tuple-element.105.kv0.kv), channel_id=1, source_target_pairs={{0,2},{1,3},{2,0},{3,1},{4,6},{5,7},{6,4},{7,5},{8,10},{9,11},{10,... | collective-permute-start | bytes 884744 | tf_op jit(solution)/shard_map/ppermute | solution.py:598
  10.4 17.3 %collective-permute-start.3 = (bf16[192,768]{1,0:T(8,128)(2,1)}, bf16[192,768]{1,0:T(8,128)(2,1)S(1)}, u32[]{:S(2)}, u32[]{:S(2)}) collective-permute-start(bf16[192,768]{1,0:T(8,128)(2,1)} %get-tuple-element.105.kv0.kv), channel_id=1, source_target_pairs={{0,1},{1,0},{2,3},{3,2},{4,5},{5,4},{6,7},{7,6},{8,9},{9,8},{10,11... | collective-permute-start | bytes 884744 | tf_op jit(solution)/shard_map/ppermute | solution.py:598
  12.2 28.4 %all-to-all-start = ((bf16[64,8,768]{2,1,0:T(8,128)(2,1)}), bf16[64,8,768]{2,1,0:T(8,128)(2,1)}, u32[]{:S(2)}, u32[]{:S(2)}) async-start(bf16[64,8,768]{2,1,0:T(8,128)(2,1)} %bitcast.5), calls=%async_computation | async-start | bytes 1572864 | tf_op jit(solution)/shard_map/all_to_all | solution.py:602
  23.4 6.8 %copy-start.4 = (bf16[192,768]{1,0:T(8,128)(2,1)}, bf16[192,768]{1,0:T(8,128)(2,1)S(1)}, u32[]{:S(2)}) copy-start(bf16[192,768]{1,0:T(8,128)(2,1)S(1)} %collective-permute-done.4.kv2) | copy-start | bytes 884740
  23.4 5.6 %collective-permute-start.5 = (bf16[192,768]{1,0:T(8,128)(2,1)S(1)}, bf16[192,768]{1,0:T(8,128)(2,1)S(1)}, u32[]{:S(2)}, u32[]{:S(2)}) collective-permute-start(bf16[192,768]{1,0:T(8,128)(2,1)S(1)} %collective-permute-done.4.kv2), channel_id=1, source_target_pairs={{0,1},{1,0},{2,3},{3,2},{4,5},{5,4},{6,7},{7,6},{8,9},{9,8},{10,11... | collective-permute-start | bytes 884744 | tf_op jit(solution)/shard_map/ppermute | solution.py:598
  24.4 17.3 %copy-start.2 = (bf16[96,768]{1,0:T(8,128)(2,1)}, bf16[96,768]{1,0:T(8,128)(2,1)S(1)}, u32[]{:S(2)}) copy-start(bf16[96,768]{1,0:T(8,128)(2,1)S(1)} %concatenate.6.rest_0_) | copy-start | bytes 442372
  24.4 16.2 %collective-permute-start.8 = (bf16[96,768]{1,0:T(8,128)(2,1)S(1)}, bf16[96,768]{1,0:T(8,128)(2,1)}, u32[]{:S(2)}, u32[]{:S(2)}) collective-permute-start(bf16[96,768]{1,0:T(8,128)(2,1)S(1)} %concatenate.6.rest_0_), channel_id=1, source_target_pairs={{0,24},{1,25},{2,26},{3,27},{4,28},{5,29},{6,30},{7,31},{8,16},{9,... | collective-permute-start | bytes 442376 | tf_op jit(solution)/shard_map/ppermute | solution.py:598
  27.0 13.7 %collective-permute-start.7 = (bf16[96,768]{1,0:T(8,128)(2,1)S(1)}, bf16[96,768]{1,0:T(8,128)(2,1)}, u32[]{:S(2)}, u32[]{:S(2)}) collective-permute-start(bf16[96,768]{1,0:T(8,128)(2,1)S(1)} %concatenate.6.rest_0_), channel_id=1, source_target_pairs={{0,16},{1,17},{2,18},{3,19},{4,20},{5,21},{6,22},{7,23},{8,24},{9,... | collective-permute-start | bytes 442376 | tf_op jit(solution)/shard_map/ppermute | solution.py:598
  27.5 13.1 %collective-permute-start.6 = (bf16[96,768]{1,0:T(8,128)(2,1)S(1)}, bf16[96,768]{1,0:T(8,128)(2,1)}, u32[]{:S(2)}, u32[]{:S(2)}) collective-permute-start(bf16[96,768]{1,0:T(8,128)(2,1)S(1)} %concatenate.6.rest_0_), channel_id=1, source_target_pairs={{0,8},{1,9},{2,10},{3,11},{4,12},{5,13},{6,14},{7,15},{8,0},{9,1},... | collective-permute-start | bytes 442376 | tf_op jit(solution)/shard_map/ppermute | solution.py:598
  27.8 2.4 %copy-start.5 = (bf16[192,768]{1,0:T(8,128)(2,1)}, bf16[192,768]{1,0:T(8,128)(2,1)S(1)}, u32[]{:S(2)}) copy-start(bf16[192,768]{1,0:T(8,128)(2,1)S(1)} %collective-permute-done.3.kv1) | copy-start | bytes 884740
  27.8 12.9 %collective-permute-start.10 = (bf16[192,768]{1,0:T(8,128)(2,1)}, bf16[192,768]{1,0:T(8,128)(2,1)}, u32[]{:S(2)}, u32[]{:S(2)}) collective-permute-start(bf16[192,768]{1,0:T(8,128)(2,1)} %get-tuple-element.92.qg.qg0), channel_id=1, source_target_pairs={{0,2},{1,3},{2,0},{3,1},{4,6},{5,7},{6,4},{7,5},{8,10},{9,11},{10,... | collective-permute-start | bytes 884744 | tf_op jit(solution)/shard_map/ppermute | solution.py:598
  29.0 1.2 %copy-start.6 = (bf16[192,768]{1,0:T(8,128)(2,1)}, bf16[192,768]{1,0:T(8,128)(2,1)S(1)}, u32[]{:S(2)}) copy-start(bf16[192,768]{1,0:T(8,128)(2,1)S(1)} %collective-permute-done.5.kv3) | copy-start | bytes 884740
  29.0 11.6 %collective-permute-start.9 = (bf16[192,768]{1,0:T(8,128)(2,1)}, bf16[192,768]{1,0:T(8,128)(2,1)}, u32[]{:S(2)}, u32[]{:S(2)}) collective-permute-start(bf16[192,768]{1,0:T(8,128)(2,1)} %get-tuple-element.92.qg.qg0), channel_id=1, source_target_pairs={{0,1},{1,0},{2,3},{3,2},{4,5},{5,4},{6,7},{7,6},{8,9},{9,8},{10,11... | collective-permute-start | bytes 884744 | tf_op jit(solution)/shard_map/ppermute | solution.py:598
  40.7 7.1 %collective-permute-start.15 = (bf16[512,768]{1,0:T(8,128)(2,1)}, bf16[512,768]{1,0:T(8,128)(2,1)}, u32[]{:S(2)}, u32[]{:S(2)}) collective-permute-start(bf16[512,768]{1,0:T(8,128)(2,1)} %bitcast.1.far_a), channel_id=1, source_target_pairs={{0,1},{1,0},{2,3},{3,2},{4,5},{5,4},{6,7},{7,6},{8,9},{9,8},{10,11... | collective-permute-start | bytes 2359304 | tf_op jit(solution)/shard_map/ppermute | solution.py:598
  41.8 2.2 %collective-permute-start.11 = (bf16[96,768]{1,0:T(8,128)(2,1)S(1)}, bf16[96,768]{1,0:T(8,128)(2,1)S(1)}, u32[]{:S(2)}, u32[]{:S(2)}) collective-permute-start(bf16[96,768]{1,0:T(8,128)(2,1)S(1)} %concatenate.6.rest_0_), channel_id=1, source_target_pairs={{0,1},{1,0},{2,3},{3,2},{4,5},{5,4},{6,7},{7,6},{8,9},{9,8},{10,11... | collective-permute-start | bytes 442376 | tf_op jit(solution)/shard_map/ppermute | solution.py:598
  41.9 2.5 %collective-permute-start.12 = (bf16[96,768]{1,0:T(8,128)(2,1)}, bf16[96,768]{1,0:T(8,128)(2,1)S(1)}, u32[]{:S(2)}, u32[]{:S(2)}) collective-permute-start(bf16[96,768]{1,0:T(8,128)(2,1)} %collective-permute-done.6.rest_1_), channel_id=1, source_target_pairs={{0,1},{1,0},{2,3},{3,2},{4,5},{5,4},{6,7},{7,6},{8,9},{9,8},{10,11... | collective-permute-start | bytes 442376 | tf_op jit(solution)/shard_map/ppermute | solution.py:598
  42.3 2.2 %collective-permute-start.13 = (bf16[96,768]{1,0:T(8,128)(2,1)}, bf16[96,768]{1,0:T(8,128)(2,1)S(1)}, u32[]{:S(2)}, u32[]{:S(2)}) collective-permute-start(bf16[96,768]{1,0:T(8,128)(2,1)} %collective-permute-done.7.rest_2_), channel_id=1, source_target_pairs={{0,1},{1,0},{2,3},{3,2},{4,5},{5,4},{6,7},{7,6},{8,9},{9,8},{10,11... | collective-permute-start | bytes 442376 | tf_op jit(solution)/shard_map/ppermute | solution.py:598
  42.4 2.4 %collective-permute-start.14 = (bf16[96,768]{1,0:T(8,128)(2,1)}, bf16[96,768]{1,0:T(8,128)(2,1)S(1)}, u32[]{:S(2)}, u32[]{:S(2)}) collective-permute-start(bf16[96,768]{1,0:T(8,128)(2,1)} %collective-permute-done.8.rest_3_), channel_id=1, source_target_pairs={{0,1},{1,0},{2,3},{3,2},{4,5},{5,4},{6,7},{7,6},{8,9},{9,8},{10,11... | collective-permute-start | bytes 442376 | tf_op jit(solution)/shard_map/ppermute | solution.py:598
  43.3 42.4 %copy-start.1 = (bf16[96,768]{1,0:T(8,128)(2,1)}, bf16[96,768]{1,0:T(8,128)(2,1)S(1)}, u32[]{:S(2)}) copy-start(bf16[96,768]{1,0:T(8,128)(2,1)S(1)} %concatenate.7.rest_0_) | copy-start | bytes 442372
  44.0 0.7 copy-start.8
  44.0 13.6 %collective-permute-start.16 = (bf16[192,768]{1,0:T(8,128)(2,1)}, bf16[192,768]{1,0:T(8,128)(2,1)S(1)}, u32[]{:S(2)}, u32[]{:S(2)}) collective-permute-start(bf16[192,768]{1,0:T(8,128)(2,1)} %collective-permute-done.10.qg2), channel_id=1, source_target_pairs={{0,1},{1,0},{2,3},{3,2},{4,5},{5,4},{6,7},{7,6},{8,9},{9,8},{10,11... | collective-permute-start | bytes 884744 | tf_op jit(solution)/shard_map/ppermute | solution.py:598
  44.4 0.7 copy-start.9
  44.5 0.7 copy-start.10
  44.7 0.7 copy-start.11
  54.3 13.4 %collective-permute-start.19 = (bf16[96,768]{1,0:T(8,128)(2,1)S(1)}, bf16[96,768]{1,0:T(8,128)(2,1)}, u32[]{:S(2)}, u32[]{:S(2)}) collective-permute-start(bf16[96,768]{1,0:T(8,128)(2,1)S(1)} %concatenate.7.rest_0_), channel_id=1, source_target_pairs={{0,24},{1,25},{2,26},{3,27},{4,28},{5,29},{6,30},{7,31},{8,16},{9,... | collective-permute-start | bytes 442376 | tf_op jit(solution)/shard_map/ppermute | solution.py:598
  55.4 26.0 %collective-permute-start.22 = (f32[32,128]{1,0:T(8,128)}, f32[32,128]{1,0:T(8,128)S(1)}, u32[]{:S(2)}, u32[]{:S(2)}) collective-permute-start(f32[32,128]{1,0:T(8,128)} %get-tuple-element.94.near_stat.st0), channel_id=1, source_target_pairs={{0,3},{1,2},{2,1},{3,0},{4,7},{5,6},{6,5},{7,4},{8,11},{9,10},{10,... | collective-permute-start | bytes 49160 | tf_op jit(solution)/shard_map/ppermute | solution.py:598
  56.6 24.8 %collective-permute-start.21 = (f32[32,128]{1,0:T(8,128)}, f32[32,128]{1,0:T(8,128)S(1)}, u32[]{:S(2)}, u32[]{:S(2)}) collective-permute-start(f32[32,128]{1,0:T(8,128)} %get-tuple-element.94.near_stat.st0), channel_id=1, source_target_pairs={{0,2},{1,3},{2,0},{3,1},{4,6},{5,7},{6,4},{7,5},{8,10},{9,11},{10,... | collective-permute-start | bytes 49160 | tf_op jit(solution)/shard_map/ppermute | solution.py:598
  57.4 24.0 %collective-permute-start.20 = (f32[32,128]{1,0:T(8,128)}, f32[32,128]{1,0:T(8,128)S(1)}, u32[]{:S(2)}, u32[]{:S(2)}) collective-permute-start(f32[32,128]{1,0:T(8,128)} %get-tuple-element.94.near_stat.st0), channel_id=1, source_target_pairs={{0,1},{1,0},{2,3},{3,2},{4,5},{5,4},{6,7},{7,6},{8,9},{9,8},{10,11... | collective-permute-start | bytes 49160 | tf_op jit(solution)/shard_map/ppermute | solution.py:598
  57.6 23.8 %copy-start.7 = (bf16[192,768]{1,0:T(8,128)(2,1)}, bf16[192,768]{1,0:T(8,128)(2,1)S(1)}, u32[]{:S(2)}) copy-start(bf16[192,768]{1,0:T(8,128)(2,1)S(1)} %collective-permute-done.16.qg3) | copy-start | bytes 884740
  57.6 23.8 %collective-permute-start.18 = (bf16[96,768]{1,0:T(8,128)(2,1)S(1)}, bf16[96,768]{1,0:T(8,128)(2,1)}, u32[]{:S(2)}, u32[]{:S(2)}) collective-permute-start(bf16[96,768]{1,0:T(8,128)(2,1)S(1)} %concatenate.7.rest_0_), channel_id=1, source_target_pairs={{0,16},{1,17},{2,18},{3,19},{4,20},{5,21},{6,22},{7,23},{8,24},{9,... | collective-permute-start | bytes 442376 | tf_op jit(solution)/shard_map/ppermute | solution.py:598
  58.3 24.0 %all-to-all-start.1 = ((bf16[64,8,768]{2,1,0:T(8,128)(2,1)}), bf16[64,8,768]{2,1,0:T(8,128)(2,1)}, u32[]{:S(2)}, u32[]{:S(2)}) async-start(bf16[64,8,768]{2,1,0:T(8,128)(2,1)} %bitcast.6), calls=%async_computation.1 | async-start | bytes 1572864 | tf_op jit(solution)/shard_map/all_to_all | solution.py:602
  67.7 13.7 %collective-permute-start.17 = (bf16[96,768]{1,0:T(8,128)(2,1)S(1)}, bf16[96,768]{1,0:T(8,128)(2,1)}, u32[]{:S(2)}, u32[]{:S(2)}) collective-permute-start(bf16[96,768]{1,0:T(8,128)(2,1)S(1)} %concatenate.7.rest_0_), channel_id=1, source_target_pairs={{0,8},{1,9},{2,10},{3,11},{4,12},{5,13},{6,14},{7,15},{8,0},{9,1},... | collective-permute-start | bytes 442376 | tf_op jit(solution)/shard_map/ppermute | solution.py:598
  81.4 5.3 %copy-start.16 = (f32[32,128]{1,0:T(8,128)}, f32[32,128]{1,0:T(8,128)S(1)}, u32[]{:S(2)}) copy-start(f32[32,128]{1,0:T(8,128)S(1)} %collective-permute-done.22.st3) | copy-start | bytes 49156
  81.4 5.3 %copy-start.17 = (f32[32,128]{1,0:T(8,128)}, f32[32,128]{1,0:T(8,128)S(1)}, u32[]{:S(2)}) copy-start(f32[32,128]{1,0:T(8,128)S(1)} %collective-permute-done.21.st2) | copy-start | bytes 49156
  81.4 5.3 %copy-start.18 = (f32[32,128]{1,0:T(8,128)}, f32[32,128]{1,0:T(8,128)S(1)}, u32[]{:S(2)}) copy-start(f32[32,128]{1,0:T(8,128)S(1)} %collective-permute-done.20.st1) | copy-start | bytes 49156
  82.2 7.7 %collective-permute-start.23 = (bf16[512,768]{1,0:T(8,128)(2,1)}, bf16[512,768]{1,0:T(8,128)(2,1)}, u32[]{:S(2)}, u32[]{:S(2)}) collective-permute-start(bf16[512,768]{1,0:T(8,128)(2,1)} %bitcast.4.far_a), channel_id=1, source_target_pairs={{0,1},{1,0},{2,3},{3,2},{4,5},{5,4},{6,7},{7,6},{8,9},{9,8},{10,11... | collective-permute-start | bytes 2359304 | tf_op jit(solution)/shard_map/ppermute | solution.py:598
  85.7 5.0 %copy-start = (s32[3,12]{1,0:T(4,128)S(1)}, s32[3,12]{1,0:T(4,128)}, u32[]{:S(2)}) copy-start(s32[3,12]{1,0:T(4,128)} %off.7) | copy-start | bytes 436
  85.7 4.1 %collective-permute-start.24 = (bf16[96,768]{1,0:T(8,128)(2,1)S(1)}, bf16[96,768]{1,0:T(8,128)(2,1)S(1)}, u32[]{:S(2)}, u32[]{:S(2)}) collective-permute-start(bf16[96,768]{1,0:T(8,128)(2,1)S(1)} %concatenate.7.rest_0_), channel_id=1, source_target_pairs={{0,1},{1,0},{2,3},{3,2},{4,5},{5,4},{6,7},{7,6},{8,9},{9,8},{10,11... | collective-permute-start | bytes 442376 | tf_op jit(solution)/shard_map/ppermute | solution.py:598
  85.8 4.1 %collective-permute-start.25 = (bf16[96,768]{1,0:T(8,128)(2,1)}, bf16[96,768]{1,0:T(8,128)(2,1)S(1)}, u32[]{:S(2)}, u32[]{:S(2)}) collective-permute-start(bf16[96,768]{1,0:T(8,128)(2,1)} %collective-permute-done.17.rest_1_), channel_id=1, source_target_pairs={{0,1},{1,0},{2,3},{3,2},{4,5},{5,4},{6,7},{7,6},{8,9},{9,8},{10,11... | collective-permute-start | bytes 442376 | tf_op jit(solution)/shard_map/ppermute | solution.py:598
  86.2 3.6 %collective-permute-start.26 = (bf16[96,768]{1,0:T(8,128)(2,1)}, bf16[96,768]{1,0:T(8,128)(2,1)S(1)}, u32[]{:S(2)}, u32[]{:S(2)}) collective-permute-start(bf16[96,768]{1,0:T(8,128)(2,1)} %collective-permute-done.18.rest_2_), channel_id=1, source_target_pairs={{0,1},{1,0},{2,3},{3,2},{4,5},{5,4},{6,7},{7,6},{8,9},{9,8},{10,11... | collective-permute-start | bytes 442376 | tf_op jit(solution)/shard_map/ppermute | solution.py:598
  86.3 3.6 %collective-permute-start.27 = (bf16[96,768]{1,0:T(8,128)(2,1)}, bf16[96,768]{1,0:T(8,128)(2,1)S(1)}, u32[]{:S(2)}, u32[]{:S(2)}) collective-permute-start(bf16[96,768]{1,0:T(8,128)(2,1)} %collective-permute-done.19.rest_3_), channel_id=1, source_target_pairs={{0,1},{1,0},{2,3},{3,2},{4,5},{5,4},{6,7},{7,6},{8,9},{9,8},{10,11... | collective-permute-start | bytes 442376 | tf_op jit(solution)/shard_map/ppermute | solution.py:598
  89.8 0.7 copy-start.13
  89.9 0.7 copy-start.14
  89.9 0.8 copy-start.15
  (1 other events, 0.7 us)

commit v2 on v1

--- a/solution.py
+++ b/solution.py
@@ -734,7 +734,6 @@
     )
 
     back_a = exchange(far_send, chip_groups)
-    near_stats = near_direct(near_stat)
     mid_qgs = plane_row(after((mid_qg,), lse)[0])
     near_qg = after((near_qg,), lse, *near_qgs)[0]
 
@@ -759,6 +758,7 @@
         offsets, queries, keys, values, grad_out, near_qg, *near_kvs, far_a, far_b, own, lse,
         delta, near_stat, *mid_kvs,
     )
+    near_stats = near_direct(after((near_stat,), grad_q)[0])
     mid_qgs = after(mid_qgs, grad_q)
     back_a = after((back_a,), *mid_qgs, *near_stats)[0]
     mid_qgs = list(mid_qgs) + [flip(x, 1) for x in mid_qgs]

time: 100 us -> 98.8 us (0.988)
  starting transfers between devices: 46 us -> 43.4 us
  waiting for transfers between devices: 5.61 us -> 6.94 us
    ppermute x28, waiting for transfers between devices: 4.85 us -> 6.93 us  [flip(): return lax.ppermute(value, 'seq', pairs)]
    ppermute x28, starting transfers between devices: 25.5 us -> 23.5 us  [flip(): return lax.ppermute(value, 'seq', pairs)]
  transfers between devices with their start and end apart: 30 -> 30, of which waited for: 5 -> 6; matrix products, arithmetic and copies ran while one was open for 1% -> 1% of each run, Pallas kernels for 31% -> 32%
where the time goes in v2:
time: 98.8 us; the launch traced here: 98.3 us
  Pallas kernels  44.1 us (45%)
  starting transfers between devices  43.4 us (44%)
  waiting for transfers between devices  6.94 us (7%)
  local copies, waits for them, and re-layouts  2.64 us (3%)
  between operations  1.17 us (1%)
    pallas_call x9, Pallas kernels, run(): return kernel(*placed)  44.1 us
    ppermute x28, starting transfers between devices, flip(): return lax.ppermute(value, 'seq', pairs)  23.5 us
    all_to_all x2, starting transfers between devices, exchange(): lax.all_to_all(value, 'seq', 0, 0, tiled=True, axis_index_groups=groups)  20 us
    ppermute x28, waiting for transfers between devices, flip(): return lax.ppermute(value, 'seq', pairs)  6.93 us
  transfers between devices with their start and end apart: 30, of which 6 were waited for; matrix products, arithmetic and copies ran while one was open for 1% of the time, Pallas kernels for 32%

profile of v2, /device:TPU:1, one launch (start us, length us, event | category | flops | bytes accessed | tf_op | source)
XLA Modules:
  0.0 98.3 jit_solution(10519471857139161820)
XLA Ops:
  0.6 4.3 %shard_map.84 = (bf16[192,768]{1,0:T(8,128)(2,1)}, bf16[192,768]{1,0:T(8,128)(2,1)}, bf16[48,768]{1,0:T(8,128)(2,1)}, bf16[512,768]{1,0:T(8,128)(2,1)}, bf16[16,...) custom-call(s32[3,12]{1,0:T(4,128)} %off.7, ...), custom_call_target="tpu_custom_call" | custom-call | flops 5000000000 | bytes 15000000 | tf_op jit(solution)/shard_map/pallas_call | solution.py:201
  5.0 3.6 %collective-permute-start.2 = (bf16[48,768]{1,0:T(8,128)(2,1)}, bf16[48,768]{1,0:T(8,128)(2,1)S(1)}, u32[]{:S(2)}, u32[]{:S(2)}) collective-permute-start(bf16[48,768]{1,0:T(8,128)(2,1)} %get-tuple-element.60), channel_id=1, source_target_pairs={{0,6},{1,7},{2,4},{3,5},{4,2},{5,3},{6,0},{7,1},{8,14},{9,15},{10,... | collective-permute-start | bytes 221192 | tf_op jit(solution)/shard_map/ppermute | solution.py:598
  8.6 0.3 collective-permute-start.1
  9.0 0.3 collective-permute-start
  9.3 1.1 %collective-permute-start.4 = (bf16[192,768]{1,0:T(8,128)(2,1)}, bf16[192,768]{1,0:T(8,128)(2,1)S(1)}, u32[]{:S(2)}, u32[]{:S(2)}) collective-permute-start(bf16[192,768]{1,0:T(8,128)(2,1)} %get-tuple-element.107.kv0.kv), channel_id=1, source_target_pairs={{0,2},{1,3},{2,0},{3,1},{4,6},{5,7},{6,4},{7,5},{8,10},{9,11},{10,... | collective-permute-start | bytes 884744 | tf_op jit(solution)/shard_map/ppermute | solution.py:598
  10.4 1.8 %collective-permute-start.3 = (bf16[192,768]{1,0:T(8,128)(2,1)}, bf16[192,768]{1,0:T(8,128)(2,1)S(1)}, u32[]{:S(2)}, u32[]{:S(2)}) collective-permute-start(bf16[192,768]{1,0:T(8,128)(2,1)} %get-tuple-element.107.kv0.kv), channel_id=1, source_target_pairs={{0,1},{1,0},{2,3},{3,2},{4,5},{5,4},{6,7},{7,6},{8,9},{9,8},{10,11... | collective-permute-start | bytes 884744 | tf_op jit(solution)/shard_map/ppermute | solution.py:598
  12.2 11.1 %all-to-all-start = ((bf16[64,8,768]{2,1,0:T(8,128)(2,1)}), bf16[64,8,768]{2,1,0:T(8,128)(2,1)}, u32[]{:S(2)}, u32[]{:S(2)}) async-start(bf16[64,8,768]{2,1,0:T(8,128)(2,1)} %bitcast.5), calls=%async_computation | async-start | bytes 1572864 | tf_op jit(solution)/shard_map/all_to_all | solution.py:602
  23.4 0.4 collective-permute-start.5
  23.8 0.6 concatenate.6.rest_0_
  24.4 2.5 %collective-permute-start.8 = (bf16[96,768]{1,0:T(8,128)(2,1)S(1)}, bf16[96,768]{1,0:T(8,128)(2,1)}, u32[]{:S(2)}, u32[]{:S(2)}) collective-permute-start(bf16[96,768]{1,0:T(8,128)(2,1)S(1)} %concatenate.6.rest_0_), channel_id=1, source_target_pairs={{0,24},{1,25},{2,26},{3,27},{4,28},{5,29},{6,30},{7,31},{8,16},{9,... | collective-permute-start | bytes 442376 | tf_op jit(solution)/shard_map/ppermute | solution.py:598
  27.0 0.6 collective-permute-start.7
  27.5 0.2 collective-permute-start.6
  27.8 1.2 %collective-permute-start.10 = (bf16[192,768]{1,0:T(8,128)(2,1)}, bf16[192,768]{1,0:T(8,128)(2,1)}, u32[]{:S(2)}, u32[]{:S(2)}) collective-permute-start(bf16[192,768]{1,0:T(8,128)(2,1)} %get-tuple-element.93.qg.qg0), channel_id=1, source_target_pairs={{0,2},{1,3},{2,0},{3,1},{4,6},{5,7},{6,4},{7,5},{8,10},{9,11},{10,... | collective-permute-start | bytes 884744 | tf_op jit(solution)/shard_map/ppermute | solution.py:598
  29.0 1.1 %collective-permute-start.9 = (bf16[192,768]{1,0:T(8,128)(2,1)}, bf16[192,768]{1,0:T(8,128)(2,1)}, u32[]{:S(2)}, u32[]{:S(2)}) collective-permute-start(bf16[192,768]{1,0:T(8,128)(2,1)} %get-tuple-element.93.qg.qg0), channel_id=1, source_target_pairs={{0,1},{1,0},{2,3},{3,2},{4,5},{5,4},{6,7},{7,6},{8,9},{9,8},{10,11... | collective-permute-start | bytes 884744 | tf_op jit(solution)/shard_map/ppermute | solution.py:598
  30.2 3.4 %shard_map.85 = (f32[768,384]{1,0:T(8,128)S(1)}, f32[16,384]{1,0:T(8,128)S(1)}, f32[16,384]{1,0:T(8,128)S(1)}) custom-call(bf16[384,768]{1,0:T(8,128)(2,1)S(1)} %get-tuple-element.58.q, bf16[384,768]{1,0:T(8,128)(2,1)S(1)} %get-tuple-element.61.k, bf16[384,768]{1,0:T(8,128)(2,1)S(1)} %get-tuple-element.62.v), custom_call_target="tpu_custom_call" | custom-call | flops 5000000000 | bytes 15000000 | tf_op jit(solution)/shard_map/pallas_call | solution.py:201
  33.6 3.3 %shard_map.86 = (f32[768,128]{1,0:T(8,128)S(1)}, f32[16,128]{1,0:T(8,128)S(1)}, f32[16,128]{1,0:T(8,128)S(1)}) custom-call(bf16[192,768]{1,0:T(8,128)(2,1)} %get-tuple-element.93.qg.qg0, bf16[192,768]{1,0:T(8,128)(2,1)} %get-tuple-element.107.kv0.kv, bf16[192,768]{1,0:T(8,128)(2,1)} %copy-done.5, bf16[192,768]{1,0:T(8,128)(2,1)} %copy-done.4, ...), custom_call_target="tpu_custom_call" | custom-call | flops 1000000000 | bytes 3000000 | tf_op jit(solution)/shard_map/pallas_call | solution.py:201
  36.8 3.8 %collective-permute-done.8.rest_3_ = bf16[96,768]{1,0:T(8,128)(2,1)} collective-permute-done((bf16[96,768]{1,0:T(8,128)(2,1)S(1)}, bf16[96,768]{1,0:T(8,128)(2,1)}, u32[]{:S(2)}, u32[]{:S(2)}) %collective-permute-start.8) | collective-permute-done | bytes 147488 | tf_op jit(solution)/shard_map/ppermute | solution.py:598
  40.7 1.1 %collective-permute-start.15 = (bf16[512,768]{1,0:T(8,128)(2,1)}, bf16[512,768]{1,0:T(8,128)(2,1)}, u32[]{:S(2)}, u32[]{:S(2)}) collective-permute-start(bf16[512,768]{1,0:T(8,128)(2,1)} %bitcast.1.far_a), channel_id=1, source_target_pairs={{0,1},{1,0},{2,3},{3,2},{4,5},{5,4},{6,7},{7,6},{8,9},{9,8},{10,11... | collective-permute-start | bytes 2359304 | tf_op jit(solution)/shard_map/ppermute | solution.py:598
  41.9 0.4 collective-permute-start.12
  42.4 0.4 collective-permute-start.14
  42.8 0.5 concatenate.7.rest_0_
  43.3 0.7 collective-permute-done.11.rest_4_
  44.0 0.4 collective-permute-start.16
  44.4 0.1 collective-permute-done.13.rest_6_
  44.5 0.2 collective-permute-done.14.rest_7_
  44.7 0.3 copy-done.9
  45.1 0.1 copy-done.10
  45.2 0.2 copy-done.11
  45.4 2.4 %shard_map.87 = (f32[16,768]{1,0:T(8,128)S(1)}, f32[1,192]{1,0:T(1,128)S(1)}, f32[1,192]{1,0:T(1,128)S(1)}) custom-call(bf16[128,768]{1,0:T(8,128)(2,1)} %get-tuple-element.83.own, bf16[96,768]{1,0:T(8,128)(2,1)} %copy-done.2, bf16[96,768]{1,0:T(8,128)(2,1)} %collective-permute-done.6.rest_1_, bf16[96,768]{1,0:T(8,128)(2,1)} %collective-permute-done.7.rest_2_, ...), custom_call_target="tpu_custom_call" | custom-call | flops 5000000000 | bytes 15000000 | tf_op jit(solution)/shard_map/pallas_call | solution.py:201
  47.8 2.8 %shard_map.88 = (f32[8,768]{1,0:T(8,128)S(1)}, f32[1,128]{1,0:T(1,128)S(1)}, f32[1,128]{1,0:T(1,128)S(1)}) custom-call(bf16[512,768]{1,0:T(8,128)(2,1)} %bitcast.1.far_a, bf16[512,768]{1,0:T(8,128)(2,1)} %collective-permute-done.15.far_b, bf16[128,768]{1,0:T(8,128)(2,1)} %get-tuple-element.83.own), custom_call_target="tpu_custom_call" | custom-call | flops 5000000000 | bytes 15000000 | tf_op jit(solution)/shard_map/pallas_call | solution.py:201
  50.6 3.7 %shard_map.89 = (bf16[384,768]{1,0:T(8,128)(2,1)}, f32[16,384]{1,0:T(8,128)S(1)}, f32[16,384]{1,0:T(8,128)S(1)}, f32[32,128]{1,0:T(8,128)}, bf16[512,768]{1,0:T(8,128)(2,1)}) custom-call(s32[3,12]{1,0:T(4,128)} %off.7, bf16[384,768]{1,0:T(8,128)(2,1)} %g_hbm.1, f32[768,384]{1,0:T(8,128)S(1)} %get-tuple-element.63.out0, ...), custom_call_target="tpu_custom_call" | custom-call | flops 5000000000 | bytes 15000000 | tf_op jit(solution)/shard_map/pallas_call | solution.py:201
  54.3 1.1 %collective-permute-start.19 = (bf16[96,768]{1,0:T(8,128)(2,1)S(1)}, bf16[96,768]{1,0:T(8,128)(2,1)}, u32[]{:S(2)}, u32[]{:S(2)}) collective-permute-start(bf16[96,768]{1,0:T(8,128)(2,1)S(1)} %concatenate.7.rest_0_), channel_id=1, source_target_pairs={{0,24},{1,25},{2,26},{3,27},{4,28},{5,29},{6,30},{7,31},{8,16},{9,... | collective-permute-start | bytes 442376 | tf_op jit(solution)/shard_map/ppermute | solution.py:598
  55.4 0.7 collective-permute-start.18
  56.1 1.5 %collective-permute-start.17 = (bf16[96,768]{1,0:T(8,128)(2,1)S(1)}, bf16[96,768]{1,0:T(8,128)(2,1)}, u32[]{:S(2)}, u32[]{:S(2)}) collective-permute-start(bf16[96,768]{1,0:T(8,128)(2,1)S(1)} %concatenate.7.rest_0_), channel_id=1, source_target_pairs={{0,8},{1,9},{2,10},{3,11},{4,12},{5,13},{6,14},{7,15},{8,0},{9,1},... | collective-permute-start | bytes 442376 | tf_op jit(solution)/shard_map/ppermute | solution.py:598
  57.6 8.9 %all-to-all-start.1 = ((bf16[64,8,768]{2,1,0:T(8,128)(2,1)}), bf16[64,8,768]{2,1,0:T(8,128)(2,1)}, u32[]{:S(2)}, u32[]{:S(2)}) async-start(bf16[64,8,768]{2,1,0:T(8,128)(2,1)} %bitcast.6), calls=%async_computation.1 | async-start | bytes 1572864 | tf_op jit(solution)/shard_map/all_to_all | solution.py:602
  66.5 12.5 %shard_map.90 = (bf16[384,768]{1,0:T(8,128)(2,1)}, f32[2304,128]{1,0:T(8,128)S(1)}, f32[2304,128]{1,0:T(8,128)S(1)}) custom-call(s32[3,12]{1,0:T(4,128)} %off.7, bf16[384,768]{1,0:T(8,128)(2,1)} %q_hbm.1, bf16[384,768]{1,0:T(8,128)(2,1)} %k_hbm.1, bf16[384,768]{1,0:T(8,128)(2,1)} %v_hbm.1, bf16[384,768]{1,0:T(8,128)(2,1)} %g_hbm.1, ...), custom_call_target="tpu_custom_call" | custom-call | flops 10000000000 | bytes 30000000 | tf_op jit(solution)/shard_map/pallas_call | solution.py:201
  79.0 2.5 %collective-permute-start.22 = (f32[32,128]{1,0:T(8,128)S(1)}, f32[32,128]{1,0:T(8,128)S(1)}, u32[]{:S(2)}, u32[]{:S(2)}) collective-permute-start(f32[32,128]{1,0:T(8,128)S(1)} %copy-done.16), channel_id=1, source_target_pairs={{0,3},{1,2},{2,1},{3,0},{4,7},{5,6},{6,5},{7,4},{8,11},{9,10},{10,... | collective-permute-start | bytes 49160 | tf_op jit(solution)/shard_map/ppermute | solution.py:598
  81.4 0.5 collective-permute-start.21
  81.9 1.2 %collective-permute-done.22.st3 = f32[32,128]{1,0:T(8,128)S(1)} collective-permute-done((f32[32,128]{1,0:T(8,128)S(1)}, f32[32,128]{1,0:T(8,128)S(1)}, u32[]{:S(2)}, u32[]{:S(2)}) %collective-permute-start.22) | collective-permute-done | bytes 16416 | tf_op jit(solution)/shard_map/ppermute | solution.py:598
  83.2 0.9 collective-permute-done.21.st2
  84.1 0.4 collective-permute-start.23
  84.5 0.2 collective-permute-start.24
  84.6 0.4 collective-permute-start.25
  85.0 0.2 collective-permute-start.26
  85.2 0.4 collective-permute-start.27
  85.5 3.1 %shard_map.91 = (f32[96,768]{1,0:T(8,128)S(1)}, f32[96,768]{1,0:T(8,128)S(1)}) custom-call(bf16[192,768]{1,0:T(8,128)(2,1)} %get-tuple-element.107.kv0.kv, bf16[192,768]{1,0:T(8,128)(2,1)} %get-tuple-element.93.qg.qg0, bf16[192,768]{1,0:T(8,128)(2,1)} %collective-permute-done.9.qg1, bf16[192,768]{1,0:T(8,128)(2,1)} %collective-permute-done.10.qg2, ...), custom_call_target="tpu_custom_call" | custom-call | flops 5000000000 | bytes 15000000 | tf_op jit(solution)/shard_map/pallas_call | solution.py:201
  88.7 0.6 copy-done.12
  89.5 8.6 %shard_map.92 = (bf16[384,768]{1,0:T(8,128)(2,1)}, bf16[384,768]{1,0:T(8,128)(2,1)}) custom-call(s32[3,12]{1,0:T(4,128)S(1)} %copy-done, s32[1]{0:T(128)} %bitcast.2.place, f32[2304,128]{1,0:T(8,128)S(1)} %get-tuple-element.97.dk0, f32[2304,128]{1,0:T(8,128)S(1)} %get-tuple-element.98.dv0, f32[96,768]{1,0:T(8,128)S(1)} %get-tuple-element.108.dk1, ...), custom_call_target="tpu_custom_call" | custom-call | flops 5000000000 | bytes 15000000 | tf_op jit(solution)/shard_map/pallas_call | solution.py:201
  (67 shorter events, 0.6 us)
Async XLA Ops:
  5.0 18.4 %copy-start.3 = (bf16[48,768]{1,0:T(8,128)(2,1)S(1)}, bf16[48,768]{1,0:T(8,128)(2,1)}, u32[]{:S(2)}) copy-start(bf16[48,768]{1,0:T(8,128)(2,1)} %get-tuple-element.60) | copy-start | bytes 221188
  5.0 18.4 %collective-permute-start.2 = (bf16[48,768]{1,0:T(8,128)(2,1)}, bf16[48,768]{1,0:T(8,128)(2,1)S(1)}, u32[]{:S(2)}, u32[]{:S(2)}) collective-permute-start(bf16[48,768]{1,0:T(8,128)(2,1)} %get-tuple-element.60), channel_id=1, source_target_pairs={{0,6},{1,7},{2,4},{3,5},{4,2},{5,3},{6,0},{7,1},{8,14},{9,15},{10,... | collective-permute-start | bytes 221192 | tf_op jit(solution)/shard_map/ppermute | solution.py:598
  8.6 15.2 %collective-permute-start.1 = (bf16[48,768]{1,0:T(8,128)(2,1)}, bf16[48,768]{1,0:T(8,128)(2,1)S(1)}, u32[]{:S(2)}, u32[]{:S(2)}) collective-permute-start(bf16[48,768]{1,0:T(8,128)(2,1)} %get-tuple-element.60), channel_id=1, source_target_pairs={{0,4},{1,5},{2,6},{3,7},{4,0},{5,1},{6,2},{7,3},{8,12},{9,13},{10,... | collective-permute-start | bytes 221192 | tf_op jit(solution)/shard_map/ppermute | solution.py:598
  9.0 14.8 %collective-permute-start = (bf16[48,768]{1,0:T(8,128)(2,1)}, bf16[48,768]{1,0:T(8,128)(2,1)S(1)}, u32[]{:S(2)}, u32[]{:S(2)}) collective-permute-start(bf16[48,768]{1,0:T(8,128)(2,1)} %get-tuple-element.60), channel_id=1, source_target_pairs={{0,2},{1,3},{2,0},{3,1},{4,6},{5,7},{6,4},{7,5},{8,10},{9,11},{10,... | collective-permute-start | bytes 221192 | tf_op jit(solution)/shard_map/ppermute | solution.py:598
  9.3 14.1 %collective-permute-start.4 = (bf16[192,768]{1,0:T(8,128)(2,1)}, bf16[192,768]{1,0:T(8,128)(2,1)S(1)}, u32[]{:S(2)}, u32[]{:S(2)}) collective-permute-start(bf16[192,768]{1,0:T(8,128)(2,1)} %get-tuple-element.107.kv0.kv), channel_id=1, source_target_pairs={{0,2},{1,3},{2,0},{3,1},{4,6},{5,7},{6,4},{7,5},{8,10},{9,11},{10,... | collective-permute-start | bytes 884744 | tf_op jit(solution)/shard_map/ppermute | solution.py:598
  10.4 17.3 %collective-permute-start.3 = (bf16[192,768]{1,0:T(8,128)(2,1)}, bf16[192,768]{1,0:T(8,128)(2,1)S(1)}, u32[]{:S(2)}, u32[]{:S(2)}) collective-permute-start(bf16[192,768]{1,0:T(8,128)(2,1)} %get-tuple-element.107.kv0.kv), channel_id=1, source_target_pairs={{0,1},{1,0},{2,3},{3,2},{4,5},{5,4},{6,7},{7,6},{8,9},{9,8},{10,11... | collective-permute-start | bytes 884744 | tf_op jit(solution)/shard_map/ppermute | solution.py:598
  12.2 28.4 %all-to-all-start = ((bf16[64,8,768]{2,1,0:T(8,128)(2,1)}), bf16[64,8,768]{2,1,0:T(8,128)(2,1)}, u32[]{:S(2)}, u32[]{:S(2)}) async-start(bf16[64,8,768]{2,1,0:T(8,128)(2,1)} %bitcast.5), calls=%async_computation | async-start | bytes 1572864 | tf_op jit(solution)/shard_map/all_to_all | solution.py:602
  23.4 6.8 %copy-start.4 = (bf16[192,768]{1,0:T(8,128)(2,1)}, bf16[192,768]{1,0:T(8,128)(2,1)S(1)}, u32[]{:S(2)}) copy-start(bf16[192,768]{1,0:T(8,128)(2,1)S(1)} %collective-permute-done.4.kv2) | copy-start | bytes 884740
  23.4 5.6 %collective-permute-start.5 = (bf16[192,768]{1,0:T(8,128)(2,1)S(1)}, bf16[192,768]{1,0:T(8,128)(2,1)S(1)}, u32[]{:S(2)}, u32[]{:S(2)}) collective-permute-start(bf16[192,768]{1,0:T(8,128)(2,1)S(1)} %collective-permute-done.4.kv2), channel_id=1, source_target_pairs={{0,1},{1,0},{2,3},{3,2},{4,5},{5,4},{6,7},{7,6},{8,9},{9,8},{10,11... | collective-permute-start | bytes 884744 | tf_op jit(solution)/shard_map/ppermute | solution.py:598
  24.4 17.3 %copy-start.2 = (bf16[96,768]{1,0:T(8,128)(2,1)}, bf16[96,768]{1,0:T(8,128)(2,1)S(1)}, u32[]{:S(2)}) copy-start(bf16[96,768]{1,0:T(8,128)(2,1)S(1)} %concatenate.6.rest_0_) | copy-start | bytes 442372
  24.4 16.2 %collective-permute-start.8 = (bf16[96,768]{1,0:T(8,128)(2,1)S(1)}, bf16[96,768]{1,0:T(8,128)(2,1)}, u32[]{:S(2)}, u32[]{:S(2)}) collective-permute-start(bf16[96,768]{1,0:T(8,128)(2,1)S(1)} %concatenate.6.rest_0_), channel_id=1, source_target_pairs={{0,24},{1,25},{2,26},{3,27},{4,28},{5,29},{6,30},{7,31},{8,16},{9,... | collective-permute-start | bytes 442376 | tf_op jit(solution)/shard_map/ppermute | solution.py:598
  27.0 13.7 %collective-permute-start.7 = (bf16[96,768]{1,0:T(8,128)(2,1)S(1)}, bf16[96,768]{1,0:T(8,128)(2,1)}, u32[]{:S(2)}, u32[]{:S(2)}) collective-permute-start(bf16[96,768]{1,0:T(8,128)(2,1)S(1)} %concatenate.6.rest_0_), channel_id=1, source_target_pairs={{0,16},{1,17},{2,18},{3,19},{4,20},{5,21},{6,22},{7,23},{8,24},{9,... | collective-permute-start | bytes 442376 | tf_op jit(solution)/shard_map/ppermute | solution.py:598
  27.5 13.1 %collective-permute-start.6 = (bf16[96,768]{1,0:T(8,128)(2,1)S(1)}, bf16[96,768]{1,0:T(8,128)(2,1)}, u32[]{:S(2)}, u32[]{:S(2)}) collective-permute-start(bf16[96,768]{1,0:T(8,128)(2,1)S(1)} %concatenate.6.rest_0_), channel_id=1, source_target_pairs={{0,8},{1,9},{2,10},{3,11},{4,12},{5,13},{6,14},{7,15},{8,0},{9,1},... | collective-permute-start | bytes 442376 | tf_op jit(solution)/shard_map/ppermute | solution.py:598
  27.8 2.4 %copy-start.5 = (bf16[192,768]{1,0:T(8,128)(2,1)}, bf16[192,768]{1,0:T(8,128)(2,1)S(1)}, u32[]{:S(2)}) copy-start(bf16[192,768]{1,0:T(8,128)(2,1)S(1)} %collective-permute-done.3.kv1) | copy-start | bytes 884740
  27.8 12.9 %collective-permute-start.10 = (bf16[192,768]{1,0:T(8,128)(2,1)}, bf16[192,768]{1,0:T(8,128)(2,1)}, u32[]{:S(2)}, u32[]{:S(2)}) collective-permute-start(bf16[192,768]{1,0:T(8,128)(2,1)} %get-tuple-element.93.qg.qg0), channel_id=1, source_target_pairs={{0,2},{1,3},{2,0},{3,1},{4,6},{5,7},{6,4},{7,5},{8,10},{9,11},{10,... | collective-permute-start | bytes 884744 | tf_op jit(solution)/shard_map/ppermute | solution.py:598
  29.0 1.2 %copy-start.6 = (bf16[192,768]{1,0:T(8,128)(2,1)}, bf16[192,768]{1,0:T(8,128)(2,1)S(1)}, u32[]{:S(2)}) copy-start(bf16[192,768]{1,0:T(8,128)(2,1)S(1)} %collective-permute-done.5.kv3) | copy-start | bytes 884740
  29.0 11.6 %collective-permute-start.9 = (bf16[192,768]{1,0:T(8,128)(2,1)}, bf16[192,768]{1,0:T(8,128)(2,1)}, u32[]{:S(2)}, u32[]{:S(2)}) collective-permute-start(bf16[192,768]{1,0:T(8,128)(2,1)} %get-tuple-element.93.qg.qg0), channel_id=1, source_target_pairs={{0,1},{1,0},{2,3},{3,2},{4,5},{5,4},{6,7},{7,6},{8,9},{9,8},{10,11... | collective-permute-start | bytes 884744 | tf_op jit(solution)/shard_map/ppermute | solution.py:598
  40.7 7.1 %collective-permute-start.15 = (bf16[512,768]{1,0:T(8,128)(2,1)}, bf16[512,768]{1,0:T(8,128)(2,1)}, u32[]{:S(2)}, u32[]{:S(2)}) collective-permute-start(bf16[512,768]{1,0:T(8,128)(2,1)} %bitcast.1.far_a), channel_id=1, source_target_pairs={{0,1},{1,0},{2,3},{3,2},{4,5},{5,4},{6,7},{7,6},{8,9},{9,8},{10,11... | collective-permute-start | bytes 2359304 | tf_op jit(solution)/shard_map/ppermute | solution.py:598
  41.8 2.2 %collective-permute-start.11 = (bf16[96,768]{1,0:T(8,128)(2,1)S(1)}, bf16[96,768]{1,0:T(8,128)(2,1)S(1)}, u32[]{:S(2)}, u32[]{:S(2)}) collective-permute-start(bf16[96,768]{1,0:T(8,128)(2,1)S(1)} %concatenate.6.rest_0_), channel_id=1, source_target_pairs={{0,1},{1,0},{2,3},{3,2},{4,5},{5,4},{6,7},{7,6},{8,9},{9,8},{10,11... | collective-permute-start | bytes 442376 | tf_op jit(solution)/shard_map/ppermute | solution.py:598
  41.9 2.5 %collective-permute-start.12 = (bf16[96,768]{1,0:T(8,128)(2,1)}, bf16[96,768]{1,0:T(8,128)(2,1)S(1)}, u32[]{:S(2)}, u32[]{:S(2)}) collective-permute-start(bf16[96,768]{1,0:T(8,128)(2,1)} %collective-permute-done.6.rest_1_), channel_id=1, source_target_pairs={{0,1},{1,0},{2,3},{3,2},{4,5},{5,4},{6,7},{7,6},{8,9},{9,8},{10,11... | collective-permute-start | bytes 442376 | tf_op jit(solution)/shard_map/ppermute | solution.py:598
  42.3 2.2 %collective-permute-start.13 = (bf16[96,768]{1,0:T(8,128)(2,1)}, bf16[96,768]{1,0:T(8,128)(2,1)S(1)}, u32[]{:S(2)}, u32[]{:S(2)}) collective-permute-start(bf16[96,768]{1,0:T(8,128)(2,1)} %collective-permute-done.7.rest_2_), channel_id=1, source_target_pairs={{0,1},{1,0},{2,3},{3,2},{4,5},{5,4},{6,7},{7,6},{8,9},{9,8},{10,11... | collective-permute-start | bytes 442376 | tf_op jit(solution)/shard_map/ppermute | solution.py:598
  42.4 2.4 %collective-permute-start.14 = (bf16[96,768]{1,0:T(8,128)(2,1)}, bf16[96,768]{1,0:T(8,128)(2,1)S(1)}, u32[]{:S(2)}, u32[]{:S(2)}) collective-permute-start(bf16[96,768]{1,0:T(8,128)(2,1)} %collective-permute-done.8.rest_3_), channel_id=1, source_target_pairs={{0,1},{1,0},{2,3},{3,2},{4,5},{5,4},{6,7},{7,6},{8,9},{9,8},{10,11... | collective-permute-start | bytes 442376 | tf_op jit(solution)/shard_map/ppermute | solution.py:598
  43.3 41.2 %copy-start.1 = (bf16[96,768]{1,0:T(8,128)(2,1)}, bf16[96,768]{1,0:T(8,128)(2,1)S(1)}, u32[]{:S(2)}) copy-start(bf16[96,768]{1,0:T(8,128)(2,1)S(1)} %concatenate.7.rest_0_) | copy-start | bytes 442372
  44.0 0.7 copy-start.8
  44.0 13.6 %collective-permute-start.16 = (bf16[192,768]{1,0:T(8,128)(2,1)}, bf16[192,768]{1,0:T(8,128)(2,1)S(1)}, u32[]{:S(2)}, u32[]{:S(2)}) collective-permute-start(bf16[192,768]{1,0:T(8,128)(2,1)} %collective-permute-done.10.qg2), channel_id=1, source_target_pairs={{0,1},{1,0},{2,3},{3,2},{4,5},{5,4},{6,7},{7,6},{8,9},{9,8},{10,11... | collective-permute-start | bytes 884744 | tf_op jit(solution)/shard_map/ppermute | solution.py:598
  44.4 0.7 copy-start.9
  44.5 0.7 copy-start.10
  54.3 27.6 %collective-permute-start.19 = (bf16[96,768]{1,0:T(8,128)(2,1)S(1)}, bf16[96,768]{1,0:T(8,128)(2,1)}, u32[]{:S(2)}, u32[]{:S(2)}) collective-permute-start(bf16[96,768]{1,0:T(8,128)(2,1)S(1)} %concatenate.7.rest_0_), channel_id=1, source_target_pairs={{0,24},{1,25},{2,26},{3,27},{4,28},{5,29},{6,30},{7,31},{8,16},{9,... | collective-permute-start | bytes 442376 | tf_op jit(solution)/shard_map/ppermute | solution.py:598
  55.4 26.5 %collective-permute-start.18 = (bf16[96,768]{1,0:T(8,128)(2,1)S(1)}, bf16[96,768]{1,0:T(8,128)(2,1)}, u32[]{:S(2)}, u32[]{:S(2)}) collective-permute-start(bf16[96,768]{1,0:T(8,128)(2,1)S(1)} %concatenate.7.rest_0_), channel_id=1, source_target_pairs={{0,16},{1,17},{2,18},{3,19},{4,20},{5,21},{6,22},{7,23},{8,24},{9,... | collective-permute-start | bytes 442376 | tf_op jit(solution)/shard_map/ppermute | solution.py:598
  56.1 25.9 %collective-permute-start.17 = (bf16[96,768]{1,0:T(8,128)(2,1)S(1)}, bf16[96,768]{1,0:T(8,128)(2,1)}, u32[]{:S(2)}, u32[]{:S(2)}) collective-permute-start(bf16[96,768]{1,0:T(8,128)(2,1)S(1)} %concatenate.7.rest_0_), channel_id=1, source_target_pairs={{0,8},{1,9},{2,10},{3,11},{4,12},{5,13},{6,14},{7,15},{8,0},{9,1},... | collective-permute-start | bytes 442376 | tf_op jit(solution)/shard_map/ppermute | solution.py:598
  57.6 21.4 %copy-start.7 = (bf16[192,768]{1,0:T(8,128)(2,1)}, bf16[192,768]{1,0:T(8,128)(2,1)S(1)}, u32[]{:S(2)}) copy-start(bf16[192,768]{1,0:T(8,128)(2,1)S(1)} %collective-permute-done.16.qg3) | copy-start | bytes 884740
  57.6 26.5 %all-to-all-start.1 = ((bf16[64,8,768]{2,1,0:T(8,128)(2,1)}), bf16[64,8,768]{2,1,0:T(8,128)(2,1)}, u32[]{:S(2)}, u32[]{:S(2)}) async-start(bf16[64,8,768]{2,1,0:T(8,128)(2,1)} %bitcast.6), calls=%async_computation.1 | async-start | bytes 1572864 | tf_op jit(solution)/shard_map/all_to_all | solution.py:602
  66.5 12.5 %copy-start.16 = (f32[32,128]{1,0:T(8,128)S(1)}, f32[32,128]{1,0:T(8,128)}, u32[]{:S(2)}) copy-start(f32[32,128]{1,0:T(8,128)} %get-tuple-element.105.near_stat.st0) | copy-start | bytes 49156
  79.0 4.2 %collective-permute-start.22 = (f32[32,128]{1,0:T(8,128)S(1)}, f32[32,128]{1,0:T(8,128)S(1)}, u32[]{:S(2)}, u32[]{:S(2)}) collective-permute-start(f32[32,128]{1,0:T(8,128)S(1)} %copy-done.16), channel_id=1, source_target_pairs={{0,3},{1,2},{2,1},{3,0},{4,7},{5,6},{6,5},{7,4},{8,11},{9,10},{10,... | collective-permute-start | bytes 49160 | tf_op jit(solution)/shard_map/ppermute | solution.py:598
  81.4 2.6 %collective-permute-start.21 = (f32[32,128]{1,0:T(8,128)S(1)}, f32[32,128]{1,0:T(8,128)S(1)}, u32[]{:S(2)}, u32[]{:S(2)}) collective-permute-start(f32[32,128]{1,0:T(8,128)S(1)} %copy-done.16), channel_id=1, source_target_pairs={{0,2},{1,3},{2,0},{3,1},{4,6},{5,7},{6,4},{7,5},{8,10},{9,11},{10,... | collective-permute-start | bytes 49160 | tf_op jit(solution)/shard_map/ppermute | solution.py:598
  81.9 2.1 %collective-permute-start.20 = (f32[32,128]{1,0:T(8,128)S(1)}, f32[32,128]{1,0:T(8,128)S(1)}, u32[]{:S(2)}, u32[]{:S(2)}) collective-permute-start(f32[32,128]{1,0:T(8,128)S(1)} %copy-done.16), channel_id=1, source_target_pairs={{0,1},{1,0},{2,3},{3,2},{4,5},{5,4},{6,7},{7,6},{8,9},{9,8},{10,11... | collective-permute-start | bytes 49160 | tf_op jit(solution)/shard_map/ppermute | solution.py:598
  83.2 2.3 %copy-start.17 = (f32[32,128]{1,0:T(8,128)}, f32[32,128]{1,0:T(8,128)S(1)}, u32[]{:S(2)}) copy-start(f32[32,128]{1,0:T(8,128)S(1)} %collective-permute-done.22.st3) | copy-start | bytes 49156
  84.0 1.5 %copy-start.18 = (f32[32,128]{1,0:T(8,128)}, f32[32,128]{1,0:T(8,128)S(1)}, u32[]{:S(2)}) copy-start(f32[32,128]{1,0:T(8,128)S(1)} %collective-permute-done.21.st2) | copy-start | bytes 49156
  84.0 1.5 %copy-start.19 = (f32[32,128]{1,0:T(8,128)}, f32[32,128]{1,0:T(8,128)S(1)}, u32[]{:S(2)}) copy-start(f32[32,128]{1,0:T(8,128)S(1)} %collective-permute-done.20.st1) | copy-start | bytes 49156
  84.1 4.7 %collective-permute-start.23 = (bf16[512,768]{1,0:T(8,128)(2,1)}, bf16[512,768]{1,0:T(8,128)(2,1)}, u32[]{:S(2)}, u32[]{:S(2)}) collective-permute-start(bf16[512,768]{1,0:T(8,128)(2,1)} %bitcast.4.far_a), channel_id=1, source_target_pairs={{0,1},{1,0},{2,3},{3,2},{4,5},{5,4},{6,7},{7,6},{8,9},{9,8},{10,11... | collective-permute-start | bytes 2359304 | tf_op jit(solution)/shard_map/ppermute | solution.py:598
  84.5 5.0 %copy-start = (s32[3,12]{1,0:T(4,128)S(1)}, s32[3,12]{1,0:T(4,128)}, u32[]{:S(2)}) copy-start(s32[3,12]{1,0:T(4,128)} %off.7) | copy-start | bytes 436
  84.5 4.1 %collective-permute-start.24 = (bf16[96,768]{1,0:T(8,128)(2,1)S(1)}, bf16[96,768]{1,0:T(8,128)(2,1)S(1)}, u32[]{:S(2)}, u32[]{:S(2)}) collective-permute-start(bf16[96,768]{1,0:T(8,128)(2,1)S(1)} %concatenate.7.rest_0_), channel_id=1, source_target_pairs={{0,1},{1,0},{2,3},{3,2},{4,5},{5,4},{6,7},{7,6},{8,9},{9,8},{10,11... | collective-permute-start | bytes 442376 | tf_op jit(solution)/shard_map/ppermute | solution.py:598
  84.6 4.0 %collective-permute-start.25 = (bf16[96,768]{1,0:T(8,128)(2,1)}, bf16[96,768]{1,0:T(8,128)(2,1)S(1)}, u32[]{:S(2)}, u32[]{:S(2)}) collective-permute-start(bf16[96,768]{1,0:T(8,128)(2,1)} %collective-permute-done.17.rest_1_), channel_id=1, source_target_pairs={{0,1},{1,0},{2,3},{3,2},{4,5},{5,4},{6,7},{7,6},{8,9},{9,8},{10,11... | collective-permute-start | bytes 442376 | tf_op jit(solution)/shard_map/ppermute | solution.py:598
  85.0 3.7 %collective-permute-start.26 = (bf16[96,768]{1,0:T(8,128)(2,1)}, bf16[96,768]{1,0:T(8,128)(2,1)S(1)}, u32[]{:S(2)}, u32[]{:S(2)}) collective-permute-start(bf16[96,768]{1,0:T(8,128)(2,1)} %collective-permute-done.18.rest_2_), channel_id=1, source_target_pairs={{0,1},{1,0},{2,3},{3,2},{4,5},{5,4},{6,7},{7,6},{8,9},{9,8},{10,11... | collective-permute-start | bytes 442376 | tf_op jit(solution)/shard_map/ppermute | solution.py:598
  85.2 3.5 %collective-permute-start.27 = (bf16[96,768]{1,0:T(8,128)(2,1)}, bf16[96,768]{1,0:T(8,128)(2,1)S(1)}, u32[]{:S(2)}, u32[]{:S(2)}) collective-permute-start(bf16[96,768]{1,0:T(8,128)(2,1)} %collective-permute-done.19.rest_3_), channel_id=1, source_target_pairs={{0,1},{1,0},{2,3},{3,2},{4,5},{5,4},{6,7},{7,6},{8,9},{9,8},{10,11... | collective-permute-start | bytes 442376 | tf_op jit(solution)/shard_map/ppermute | solution.py:598
  88.6 0.7 copy-start.13
  88.7 0.7 copy-start.14
  88.7 0.8 copy-start.15
  (2 other events, 1.3 us)
